TPU v7x, 1024 devices: a whole 4x4x32 slice. The times are simulated.
1024 devices in a mesh: rep: 64 (over z, core), tp: 16 (over y, x).
Axes of the slice: x: 4, y: 4, z: 32, core: 2. Of those that a mesh axis runs over, the one named last changes fastest.
Arguments:
- tokens: bfloat16 [3072, 3072], P('rep', 'tp'), may hold values from -6 to 6
- routes: int32 [3072, 4], P('rep'), may hold values from 0 to 31, all different within a row; in each aligned block of 48 rows (0 to 47, 48 to 95, ...) at most 12 rows name the same one
- gates: float32 [3072, 4], P('rep'), may hold values from 0.1 to 1
- w_gate: bfloat16 [64, 3072, 3072], P('rep', None, 'tp'), may hold values from -0.109375 to 0.109375
- w_up: bfloat16 [64, 3072, 3072], P('rep', None, 'tp'), may hold values from -0.109375 to 0.109375
- w_down: bfloat16 [64, 3072, 3072], P('rep', 'tp'), may hold values from -0.078125 to 0.078125
Outputs:
- mixed: bfloat16 [3072, 3072], P('rep', 'tp')
Inputs may be any that keep to these rules, and one draw needn't show every extreme that they name: `routes`: A token's 4 slots are different. Among the 48 tokens of one index of rep, no slot is named by more than 12 choices, a bound that some block reaches.
All inputs are finite; a program needn't handle non-finite values.
Results may differ from a plain program's by a relative error of at most 0.019.
Values may be sent and summed in bfloat16 or wider, within the bound.
No kernel may reach another device: no remote copies, remote signals or barrier semaphores. Data moves between devices by JAX's collectives and lax.ppermute only.
A program may use at most 32 MiB of HBM per device.

v0:
```python
import jax
import jax.numpy as jnp
from jax import lax
from jax.sharding import PartitionSpec as P


def per_device(tokens, routes, gates, w_gate, w_up, w_down):
    replicas = lax.axis_size("rep")
    slot_count = replicas // 2
    tok_count = tokens.shape[0]
    top_count = routes.shape[1]
    share = tokens.shape[1]
    capacity = min(tok_count, 2 * tok_count * top_count // slot_count)
    entries = tok_count * top_count
    flat_slot = routes.reshape(-1)
    onehot = (flat_slot[:, None] == jnp.arange(slot_count, dtype=jnp.int32)[None, :]).astype(
        jnp.int32
    )
    before = jnp.cumsum(onehot, axis=0) - onehot
    position = jnp.sum(before * onehot, axis=1)
    target = flat_slot * capacity + position
    places = jnp.arange(slot_count * capacity, dtype=jnp.int32)
    matches = target[None, :] == places[:, None]
    source = jnp.sum(jnp.where(matches, jnp.arange(entries, dtype=jnp.int32)[None, :], 0), axis=1)
    filled = jnp.any(matches, axis=1)
    outgoing = jnp.where(filled[:, None], tokens[source // top_count], jnp.zeros((), jnp.bfloat16))
    outgoing = outgoing.reshape(slot_count, capacity, share)
    outgoing = jnp.repeat(outgoing, 2, axis=0)
    gate_mat = w_gate[0]
    up_mat = w_up[0]
    down_mat = w_down[0]
    incoming = lax.all_to_all(outgoing, "rep", split_axis=0, concat_axis=0, tiled=True)
    row_data = incoming.reshape(-1, share)
    full_rows = lax.all_gather(row_data, "tp", axis=1, tiled=True)
    gate_acc = jnp.dot(full_rows, gate_mat, preferred_element_type=jnp.float32)
    up_acc = jnp.dot(full_rows, up_mat, preferred_element_type=jnp.float32)
    hidden = (jax.nn.silu(gate_acc) * up_acc).astype(jnp.bfloat16)
    partial_value = jnp.dot(hidden, down_mat, preferred_element_type=jnp.float32).astype(
        jnp.bfloat16
    )
    summed = lax.psum_scatter(
        partial_value.astype(jnp.float32).astype(jnp.bfloat16),
        "tp",
        scatter_dimension=1,
        tiled=True,
    )
    returned = lax.all_to_all(
        summed.reshape(incoming.shape), "rep", split_axis=0, concat_axis=0, tiled=True
    )
    halves = returned.reshape(slot_count, 2, capacity, share).astype(jnp.float32)
    combined = (halves[:, 0] + halves[:, 1]).reshape(-1, share)
    picked = combined[target].reshape(tok_count, top_count, share)
    mixed = jnp.sum(gates[:, :, None] * picked, axis=1)
    return mixed.astype(jnp.bfloat16)


def solution(mesh):
    in_specs = (
        P("rep", "tp"),
        P("rep", None),
        P("rep", None),
        P("rep", None, "tp"),
        P("rep", None, "tp"),
        P("rep", "tp", None),
    )
    out_specs = P("rep", "tp")
    return jax.shard_map(
        per_device, mesh=mesh, in_specs=in_specs, out_specs=out_specs, check_vma=False
    )
```

profile of v0, /device:TPU:6, one launch (start us, length us, event | category | flops | bytes accessed | tf_op | source)
XLA Modules:
  0.0 403.5 jit_solution(17430643031728295492)
XLA Ops:
  6.5 0.0 copy-start
  6.5 0.0 copy-start.1
  6.5 0.0 all-gather.2.cloned.1.call-start
  6.5 0.9 copy.28
  7.4 0.1 reshape.137
  7.5 0.6 reduce-window.6
  8.1 0.2 slice_reduce_fusion
  8.4 0.1 bitcast_bitcast_fusion
  8.5 0.1 select_reduce_fusion
  8.6 0.1 fusion.14
  8.8 0.0 copy-done.1
  8.8 2.1 gather_fusion
  10.9 0.1 gather.9
  10.9 0.1 broadcast_in_dim.37
  11.0 0.1 broadcast_select_fusion
  11.2 94.9 %all_to_all.10 = bf16[64,12,192]{2,1,0:T(8,128)(2,1)S(1)} all-to-all(bf16[64,12,192]{2,1,0:T(8,128)(2,1)S(1)} %bitcast.41), channel_id=1, replica_groups=mesh['rep'=64,'tp'=16] {'rep'}, dimensions={0} | all-to-all | bytes 589824 | tf_op jit(solution)/shard_map/all_to_all | solution.py:32
  106.1 0.0 copy-start.2
  106.1 0.2 reshape.141
  106.3 0.9 copy.31
  107.2 0.0 all-gather.2.cloned.1.call-update
  107.2 0.0 reduce-scatter.2.cloned.1.call-start
  107.3 71.0 %all-gather.2.cloned.1.call-done = bf16[768,3072]{0,1:T(8,128)(2,1)} async-done(((bf16[768,192]{0,1:T(8,128)(2,1)}), bf16[768,3072]{0,1:T(8,128)(2,1)}) %all-gather.2.cloned.1.call-update) | async-done | bytes 4718608 | tf_op jit(solution)/shard_map/all_gather | solution.py:34
  178.2 0.0 copy-done.2
  178.2 3.4 fusion.3
  181.7 0.0 copy-done
  181.7 7.3 %convolution_convert_fusion = bf16[768,3072]{0,1:T(8,128)(2,1)} fusion(bf16[1,192,3072]{2,1,0:T(8,128)(2,1)S(1)} %copy-done, bf16[768,3072]{0,1:T(8,128)(2,1)} %all-gather.2.cloned.1.call-done, bf16[1,3072,192]{1,2,0:T(8,128)(2,1)} %param.10, f32[768,192]{0,1:T(8,128)S(1)} %fusion.3), kind=kOutput, calls=%fused_computation.2 | convolution fusion | flops 1815183360 | bytes 12386304 | tf_op jit(solution)/shard_map/dot_general | solution.py:38
  189.0 0.0 reduce-scatter.2.cloned.1.call-update
  189.0 0.0 copy-start.3
  189.0 114.4 %reduce-scatter.2.cloned.1.call-done = bf16[768,192]{0,1:T(8,128)(2,1)} async-done(((bf16[768,3072]{0,1:T(8,128)(2,1)}), bf16[768,192]{0,1:T(8,128)(2,1)}) %reduce-scatter.2.cloned.1.call-update) | async-done | bytes 294928 | tf_op jit(solution)/shard_map/reduce_scatter | solution.py:41
  303.5 1.1 copy.32
  304.6 0.0 copy-start.4
  304.6 0.9 reshape.142
  305.5 23.4 %all-to-all-start.1 = ((bf16[64,12,192]{2,1,0:T(8,128)(2,1)}), bf16[64,12,192]{2,1,0:T(8,128)(2,1)S(1)}, u32[]{:S(2)}, u32[]{:S(2)}) async-start(bf16[64,12,192]{2,1,0:T(8,128)(2,1)} %reshape.142), calls=%async_computation.2 | async-start | bytes 1048576 | tf_op jit(solution)/shard_map/all_to_all | solution.py:47
  328.9 0.0 copy-done.3
  328.9 0.1 copy.35
  329.0 0.1 mul.50
  329.1 0.0 copy-done.4
  329.1 0.1 copy.27
  329.2 65.4 %all-to-all-done.1 = bf16[64,12,192]{2,1,0:T(8,128)(2,1)S(1)} async-done(((bf16[64,12,192]{2,1,0:T(8,128)(2,1)}), bf16[64,12,192]{2,1,0:T(8,128)(2,1)S(1)}, u32[]{:S(2)}, u32[]{:S(2)}) %all-to-all-start.1) | async-done | bytes 294944 | tf_op jit(solution)/shard_map/all_to_all | solution.py:47
  394.6 0.1 convert.8
  394.8 0.1 fusion.12
  394.9 0.9 gather_fusion.1
  395.8 0.1 reshape.143
  395.9 0.8 multiply_reduce_fusion
  (13 shorter events, 0.2 us)
Async XLA Ops:
  6.5 175.2 %copy-start = (bf16[1,192,3072]{2,1,0:T(8,128)(2,1)S(1)}, bf16[1,192,3072]{2,1,0:T(8,128)(2,1)}, u32[]{:S(2)}) copy-start(bf16[1,192,3072]{2,1,0:T(8,128)(2,1)} %param.11) | copy-start | bytes 3538948
  6.5 2.2 copy-start.1
  6.5 171.7 %all-gather.2.cloned.1.call-start = ((), (), s32[]{:S(2)}) async-start(), calls=%async_computation.3 | async-start | bytes 5013504 | tf_op jit(solution)/shard_map/all_gather | solution.py:34
  106.1 72.1 %copy-start.2 = (bf16[1,3072,192]{1,2,0:T(8,128)(2,1)S(1)}, bf16[1,3072,192]{1,2,0:T(8,128)(2,1)}, u32[]{:S(2)}) copy-start(bf16[1,3072,192]{1,2,0:T(8,128)(2,1)} %param.9) | copy-start | bytes 3538948
  107.2 196.2 %reduce-scatter.2.cloned.1.call-start = ((), (), s32[]{:S(2)}) async-start(), calls=%async_computation.4 | async-start | bytes 5013504 | tf_op jit(solution)/shard_map/reduce_scatter | solution.py:41
  189.0 139.9 %copy-start.3 = (s32[48,4]{0,1:T(4,128)S(1)}, s32[48,4]{0,1:T(4,128)}, u32[]{:S(2)}) copy-start(s32[48,4]{0,1:T(4,128)} %param.7) | copy-start | bytes 2308
  304.6 24.5 %copy-start.4 = (f32[48,4]{0,1:T(4,128)S(1)}, f32[48,4]{0,1:T(4,128)}, u32[]{:S(2)}) copy-start(f32[48,4]{0,1:T(4,128)} %param.8) | copy-start | bytes 2308
  305.5 89.1 %all-to-all-start.1 = ((bf16[64,12,192]{2,1,0:T(8,128)(2,1)}), bf16[64,12,192]{2,1,0:T(8,128)(2,1)S(1)}, u32[]{:S(2)}, u32[]{:S(2)}) async-start(bf16[64,12,192]{2,1,0:T(8,128)(2,1)} %reshape.142), calls=%async_computation.2 | async-start | bytes 1048576 | tf_op jit(solution)/shard_map/all_to_all | solution.py:47
Sparse Core Ops, SparseCore 0:
  107.3 70.8 all-gather.1
  189.2 114.2 reduce-scatter.1
where the time goes:
time: 404 us
  waiting for transfers between devices  251 us (62%)
  blocking collectives  94.9 us (23%)
  starting transfers between devices  23.4 us (6%)
  between operations  13.6 us (3%)
  matrix products  10.7 us (3%)
  local copies, waits for them, and re-layouts  7.79 us (2%)
    reduce_scatter x1, waiting for transfers between devices, per_device(): lax.psum_scatter(partial_value.astype(jnp.float32).astype(jnp.bfloat16),...  114 us
    all_to_all x1, blocking collectives, per_device(): lax.all_to_all(outgoing, 'rep', split_axis=0, concat_axis=0, tiled=True)  94.9 us
    all_gather x1, waiting for transfers between devices, per_device(): full_rows = lax.all_gather(row_data, 'tp', axis=1, tiled=True)  71 us
    all_to_all x1, waiting for transfers between devices, per_device(): lax.all_to_all(summed.reshape(incoming.shape), 'rep', split_axis=0, conca...  65.4 us
    all_to_all x1, starting transfers between devices, per_device(): lax.all_to_all(summed.reshape(incoming.shape), 'rep', split_axis=0, conca...  23.4 us
  transfers between devices with their start and end apart: 3, of which 3 were waited for; matrix products, arithmetic and copies ran while one was open for 0% of the time, Pallas kernels for 0%

commit v1 on v0

v1 whole, which is shorter than its diff:
```python
import functools

import jax
import jax.numpy as jnp
from jax import lax
from jax.experimental import pallas as pl
from jax.experimental.pallas import tpu as pltpu
from jax.sharding import Mesh
from jax.sharding import PartitionSpec as P

LANES = 128
HALF = LANES // 2
SHARE = LANES + HALF
F32 = jnp.float32
BF16 = jnp.bfloat16


def iota(shape, dim):
    return lax.broadcasted_iota(jnp.int32, shape, dim)


def lines_of(slot, place, cap):
    half, lines = cap // 2, 3 * cap // 2
    start = slot * lines
    head = start + place
    low = jnp.where(place < half, start + cap + place, -1)
    high = jnp.where(place < half, -1, start + cap + place - half)
    return head, low, high


def dispatch_kernel(slots, cap, tokens_ref, routes_ref, out_ref):
    odd = lax.rem(lax.axis_index("x"), 2) == 1
    count = tokens_ref.shape[0]
    top = routes_ref.shape[0]
    total = slots * cap * 3 // 2
    tok = tokens_ref[...].astype(F32)
    head = jnp.where(odd, tok[:, HALF:], tok[:, :LANES])
    tail = jnp.where(odd, tok[:, :HALF], tok[:, LANES:])
    both = jnp.concatenate([tail, tail], axis=1)
    left = iota((count, LANES), 1) < HALF
    chosen = [routes_ref[k : k + 1, :] for k in range(top)]
    slot_ids = iota((slots, count), 0)
    onehots = [chosen[k] == slot_ids for k in range(top)]
    named = functools.reduce(jnp.logical_or, onehots).astype(F32).astype(BF16)
    earlier = (iota((count, count), 0) < iota((count, count), 1)).astype(F32).astype(BF16)
    before = jnp.dot(named, earlier, preferred_element_type=F32)
    line_ids = iota((total, count), 0)
    masks = [None, None, None]
    for k in range(top):
        place = jnp.sum(jnp.where(onehots[k], before, 0.0), axis=0, keepdims=True).astype(jnp.int32)
        for n, line in enumerate(lines_of(chosen[k], place, cap)):
            hit = line_ids == line
            masks[n] = hit if masks[n] is None else jnp.logical_or(masks[n], hit)
    parts = (head, jnp.where(left, both, 0.0), jnp.where(left, 0.0, both))
    out = jnp.zeros((total, LANES), F32)
    for mask, part in zip(masks, parts):
        out = out + jnp.dot(
            mask.astype(F32).astype(BF16), part.astype(BF16), preferred_element_type=F32
        )
    out_ref[...] = out.astype(BF16)


def spread_kernel(cap, in_ref, out_ref):
    total = in_ref.shape[0]
    half, group = cap // 2, in_ref.shape[0] // 3
    place = iota((total, 1), 0)
    kind, rest = place // group, place % group
    source = rest // half * (3 * half) + rest % half + kind * half
    order = (source == iota((total, total), 1)).astype(F32).astype(BF16)
    lines = jnp.dot(order, in_ref[...], preferred_element_type=F32).astype(BF16)
    for n in range(out_ref.shape[0]):
        out_ref[n] = lines


def ffn_kernel(x_ref, gate_ref, up_ref, down_ref, out_ref, rows_ref):
    rows = rows_ref.shape[0]
    mid = rows // 2
    left = iota((mid, LANES), 1) < HALF
    pairs = x_ref.shape[0] // 2
    wide = 3 * LANES
    for n in range(pairs):
        start = n * wide
        rows_ref[:, start : start + LANES] = x_ref[2 * n, :rows, :]
        rows_ref[:, start + 2 * LANES : start + wide] = x_ref[2 * n + 1, :rows, :]
        a = x_ref[2 * n, rows:, :].astype(F32)
        b = x_ref[2 * n + 1, rows:, :].astype(F32)
        upper = jnp.where(left, a, pltpu.roll(b, HALF, 1))
        lower = jnp.where(left, pltpu.roll(a, HALF, 1), b)
        rows_ref[:mid, start + LANES : start + 2 * LANES] = upper.astype(BF16)
        rows_ref[mid:, start + LANES : start + 2 * LANES] = lower.astype(BF16)
    hidden = []
    last = (((1,), (1,)), ((), ()))
    for h in range(2):
        gate = lax.dot_general(rows_ref[...], gate_ref[h], last, preferred_element_type=F32)
        up = lax.dot_general(rows_ref[...], up_ref[h], last, preferred_element_type=F32)
        hidden.append((gate / (1.0 + jnp.exp(-gate)) * up).astype(BF16))
    for n in range(pairs):
        start = n * wide
        out = jnp.dot(hidden[0], down_ref[0, :, start : start + wide], preferred_element_type=F32)
        out = out + jnp.dot(
            hidden[1], down_ref[1, :, start : start + wide], preferred_element_type=F32
        )
        out_ref[2 * n, :rows, :] = out[:, :LANES].astype(BF16)
        out_ref[2 * n + 1, :rows, :] = out[:, 2 * LANES :].astype(BF16)
        upper, lower = out[:mid, LANES : 2 * LANES], out[mid:, LANES : 2 * LANES]
        out_ref[2 * n, rows:, :] = jnp.where(left, upper, pltpu.roll(lower, HALF, 1)).astype(BF16)
        out_ref[2 * n + 1, rows:, :] = jnp.where(left, pltpu.roll(upper, HALF, 1), lower).astype(
            BF16
        )


def sum_kernel(cap, in_ref, out_ref):
    total = in_ref.shape[1]
    half, group = cap // 2, total // 3
    acc = in_ref[0].astype(F32)
    for n in range(1, in_ref.shape[0]):
        acc = acc + in_ref[n].astype(F32)
    place = iota((total, 1), 0)
    block, line = place // (3 * half), place % (3 * half)
    source = line // half * group + block * half + line % half
    order = (source == iota((total, total), 1)).astype(F32).astype(BF16)
    out_ref[...] = jnp.dot(order, acc.astype(BF16), preferred_element_type=F32).astype(BF16)


def combine_kernel(slots, cap, in_ref, routes_ref, gates_ref, out_ref):
    odd = lax.rem(lax.axis_index("x"), 2) == 1
    count, top = routes_ref.shape
    total = in_ref.shape[0]
    slot_ids = iota((count, slots), 1)
    chosen = [routes_ref[:, k : k + 1] for k in range(top)]
    onehots = [chosen[k] == slot_ids for k in range(top)]
    named = functools.reduce(jnp.logical_or, onehots).astype(F32).astype(BF16)
    earlier = (iota((count, count), 0) > iota((count, count), 1)).astype(F32).astype(BF16)
    before = jnp.dot(earlier, named, preferred_element_type=F32)
    line_ids = iota((count, total), 1)
    weights = [jnp.zeros((count, total), F32) for _ in range(3)]
    for k in range(top):
        place = jnp.sum(jnp.where(onehots[k], before, 0.0), axis=1, keepdims=True).astype(jnp.int32)
        for n, line in enumerate(lines_of(chosen[k], place, cap)):
            weights[n] = jnp.where(line_ids == line, gates_ref[:, k : k + 1], weights[n])
    lines = in_ref[...]
    sums = []
    for weight in weights:
        coarse = weight.astype(BF16)
        fine = (weight - coarse.astype(F32)).astype(BF16)
        sums.append(
            jnp.dot(coarse, lines, preferred_element_type=F32)
            + jnp.dot(fine, lines, preferred_element_type=F32)
        )
    head, tail = sums[0], sums[1][:, :HALF] + sums[2][:, HALF:]
    out = jnp.where(
        odd, jnp.concatenate([tail, head], axis=1), jnp.concatenate([head, tail], axis=1)
    )
    out_ref[...] = out.astype(BF16)


def call(kernel, shape, *args, scratch=(), limit=16, flops=0):
    vmem = pl.BlockSpec(memory_space=pltpu.VMEM)
    size = sum(a.size * a.dtype.itemsize for a in args)
    return pl.pallas_call(
        kernel,
        out_shape=jax.ShapeDtypeStruct(shape, BF16),
        in_specs=[vmem] * len(args),
        out_specs=vmem,
        scratch_shapes=list(scratch),
        compiler_params=pltpu.CompilerParams(vmem_limit_bytes=limit * 1024 * 1024),
        cost_estimate=pl.CostEstimate(flops=flops, bytes_accessed=size, transcendentals=0),
    )(*args)


def exchange_z(lines, slots):
    blocks = lines.reshape(slots, -1, 2, LANES)
    return lax.all_to_all(blocks, "z", split_axis=0, concat_axis=0, tiled=True).reshape(lines.shape)


def per_device(tokens, routes, gates, w_gate, w_up, w_down):
    slots = lax.axis_size("z")
    shares = lax.axis_size("y") * lax.axis_size("x")
    count, top = routes.shape
    cap = min(count, 2 * count * top // slots)
    total = slots * cap * 3 // 2
    rows = slots * cap
    gate_all = lax.all_gather(w_gate.swapaxes(1, 2), "core", axis=0, tiled=True)
    up_all = lax.all_gather(w_up.swapaxes(1, 2), "core", axis=0, tiled=True)
    down_all = lax.all_gather(w_down, "core", axis=0, tiled=True)
    outgoing = call(
        functools.partial(dispatch_kernel, slots, cap), (total, LANES), tokens, routes.T
    )
    incoming = exchange_z(outgoing, slots)
    copies = call(functools.partial(spread_kernel, cap), (shares, total, LANES), incoming)
    features = lax.all_to_all(copies, ("y", "x"), split_axis=0, concat_axis=0, tiled=True)
    partials = call(
        ffn_kernel,
        (shares, total, LANES),
        features,
        gate_all,
        up_all,
        down_all,
        scratch=[pltpu.VMEM((rows, shares * SHARE), BF16)],
        limit=40,
        flops=2 * rows * shares * SHARE * 6 * SHARE,
    )
    landed = lax.all_to_all(partials, ("y", "x"), split_axis=0, concat_axis=0, tiled=True)
    summed = call(functools.partial(sum_kernel, cap), (total, LANES), landed)
    returned = exchange_z(summed, slots)
    return call(
        functools.partial(combine_kernel, slots, cap), (count, SHARE), returned, routes, gates
    )


def split_mesh(mesh):
    reps, shares = mesh.devices.shape
    side = int(round(shares**0.5))
    return Mesh(mesh.devices.reshape(reps // 2, 2, side, -1), ("z", "core", "y", "x"))


def solution(mesh):
    rep, tp = ("z", "core"), ("y", "x")
    in_specs = (
        P(rep, tp),
        P(rep, None),
        P(rep, None),
        P(rep, None, tp),
        P(rep, None, tp),
        P(rep, tp, None),
    )
    return jax.shard_map(
        per_device,
        mesh=split_mesh(mesh),
        in_specs=in_specs,
        out_specs=P(rep, tp),
        check_vma=False,
    )
```

time: 404 us -> 232 us (0.57)
  waiting for transfers between devices: 251 us -> 106 us
  blocking collectives: 94.9 us -> 36.2 us
  starting transfers between devices: 23.4 us -> 59.1 us
  Pallas kernels: 0 us -> 11 us
  matrix products: 10.7 us -> 0 us
    reduce_scatter x1 -> x0, waiting for transfers between devices: 114 us -> none  [per_device(): lax.psum_scatter(partial_value.astype(jnp.float32).astype(jnp.bfloat16),...]
    all_to_all x1, blocking collectives: 94.9 us -> 36.2 us  [per_device(): lax.all_to_all(partials, ('y', 'x'), split_axis=0, concat_axis=0, tiled=T...]
    all_to_all x1 -> x3, starting transfers between devices: 23.4 us -> 59.1 us  [the longest x2 51.6 us: exchange_z(): lax.all_to_all(blocks, 'z', split_axis=0, concat_axis=0, tiled=True)]
    all_gather x1 -> x3, waiting for transfers between devices: 71 us -> 40.1 us  [the longest x1 35.8 us: per_device(): down_all = lax.all_gather(w_down, 'core', axis=0, tiled=True)]
    pallas_call x0 -> x5, Pallas kernels: none -> 11 us  [call(): pl.pallas_call(kernel, out_shape=jax.ShapeDtypeStruct(shape, BF16), in_sp...]
    dot_general x2 -> x0, matrix products: 10.7 us -> none  [the longest x1 7.3 us: per_device(): jnp.dot(hidden, down_mat, preferred_element_type=jnp.float32)]
    unnamed x12 -> x14, local copies, waits for them, and re-layouts: 0.99 us -> 5.19 us
    all_to_all x1 -> x3, waiting for transfers between devices: 65.4 us -> 63.8 us  [the longest x2 63.8 us: exchange_z(): lax.all_to_all(blocks, 'z', split_axis=0, concat_axis=0, tiled=True)]
  transfers between devices with their start and end apart: 3 -> 6, of which waited for: 3 -> 4; matrix products, arithmetic and copies ran while one was open for 0% -> 0% of each run, Pallas kernels for 0% -> 2%
where the time goes in v1:
time: 232 us; the launch traced here: 231 us
  waiting for transfers between devices  106 us (46%)
  starting transfers between devices  59.1 us (25%)
  blocking collectives  36.2 us (16%)
  between operations  13.2 us (6%)
  Pallas kernels  11 us (5%)
  local copies, waits for them, and re-layouts  5.19 us (2%)
    all_to_all x2, waiting for transfers between devices, exchange_z(): lax.all_to_all(blocks, 'z', split_axis=0, concat_axis=0, tiled=True)  63.8 us
    all_to_all x2, starting transfers between devices, exchange_z(): lax.all_to_all(blocks, 'z', split_axis=0, concat_axis=0, tiled=True)  51.6 us
    all_to_all x1, blocking collectives, per_device(): lax.all_to_all(partials, ('y', 'x'), split_axis=0, concat_axis=0, tiled=T...  36.2 us
    all_gather x1, waiting for transfers between devices, per_device(): down_all = lax.all_gather(w_down, 'core', axis=0, tiled=True)  35.8 us
    pallas_call x5, Pallas kernels, call(): pl.pallas_call(kernel, out_shape=jax.ShapeDtypeStruct(shape, BF16), in_sp...  11 us
    all_to_all x1, starting transfers between devices, per_device(): lax.all_to_all(copies, ('y', 'x'), split_axis=0, concat_axis=0, tiled=True)  7.42 us
    unnamed x14, local copies, waits for them, and re-layouts  5.19 us
  transfers between devices with their start and end apart: 6, of which 4 were waited for; matrix products, arithmetic and copies ran while one was open for 0% of the time, Pallas kernels for 2%

profile of v1, /device:TPU:6, one launch (start us, length us, event | category | flops | bytes accessed | tf_op | source)
XLA Modules:
  0.0 230.7 jit_solution(1572470178293057720)
XLA Ops:
  6.5 0.0 copy-start.4
  6.5 0.0 copy-start.3
  6.5 0.0 all-gather.4.cloned.1.call-start
  6.5 0.7 all-gather.4.cloned.1.call-update
  7.3 0.0 all-gather.6.cloned.1.call-start
  7.3 0.7 all-gather.6.cloned.1.call-update
  8.0 0.0 copy-done.4
  8.0 0.0 copy-done.3
  8.0 1.3 shard_map.64
  9.3 28.7 %all-to-all-start = ((bf16[32,9,2,128]{3,2,1,0:T(2,128)(2,1)}), bf16[32,9,2,128]{3,2,1,0:T(2,128)(2,1)S(1)}, u32[]{:S(2)}, u32[]{:S(2)}) async-start(bf16[32,9,2,128]{3,2,1,0:T(2,128)(2,1)} %bitcast.1), calls=%async_computation | async-start | bytes 294912 | tf_op jit(solution)/shard_map/all_to_all | solution.py:173
  38.1 0.0 all-gather.8.cloned.1.call-start
  38.1 0.7 all-gather.8.cloned.1.call-update
  38.8 32.1 %all-to-all-done = bf16[32,9,2,128]{3,2,1,0:T(2,128)(2,1)S(1)} async-done(((bf16[32,9,2,128]{3,2,1,0:T(2,128)(2,1)}), bf16[32,9,2,128]{3,2,1,0:T(2,128)(2,1)S(1)}, u32[]{:S(2)}, u32[]{:S(2)}) %all-to-all-start) | async-done | bytes 147488 | tf_op jit(solution)/shard_map/all_to_all | solution.py:173
  70.9 2.3 shard_map.65
  73.2 7.4 %all-to-all-start.1 = ((bf16[16,576,128]{2,1,0:T(8,128)(2,1)}), bf16[16,576,128]{2,1,0:T(8,128)(2,1)S(1)}, u32[]{:S(2)}, u32[]{:S(2)}) async-start(bf16[16,576,128]{2,1,0:T(8,128)(2,1)} %shard_map.65), calls=%async_computation.1 | async-start | bytes 4718592 | tf_op jit(solution)/shard_map/all_to_all | solution.py:191
  80.7 0.0 all-gather.4.cloned.1.call-done.gate_ref
  80.7 4.3 %all-gather.6.cloned.1.call-done.up_ref = bf16[2,192,3072]{2,1,0:T(8,128)(2,1)} async-done(((bf16[1,192,3072]{2,1,0:T(8,128)(2,1)}), bf16[2,192,3072]{2,1,0:T(8,128)(2,1)}) %all-gather.6.cloned.1.call-update) | async-done | bytes 2359312 | tf_op jit(solution)/shard_map/all_gather | solution.py:184
  84.9 35.8 %all-gather.8.cloned.1.call-done.down_ref = bf16[2,192,3072]{2,1,0:T(8,128)(2,1)} async-done(((bf16[1,192,3072]{2,1,0:T(8,128)(2,1)}), bf16[2,192,3072]{2,1,0:T(8,128)(2,1)}) %all-gather.8.cloned.1.call-update) | async-done | bytes 2359312 | tf_op jit(solution)/shard_map/all_gather | solution.py:185
  120.8 0.0 all-to-all-done.1.x_ref
  120.8 0.0 copy-start
  120.8 1.7 copy-done
  122.4 0.0 copy-start.1
  122.4 1.7 copy-done.1
  124.1 0.0 copy-start.2
  124.1 1.7 copy-done.2
  125.8 4.4 %shard_map.66 = bf16[16,576,128]{2,1,0:T(8,128)(2,1)S(1)} custom-call(bf16[16,576,128]{2,1,0:T(8,128)(2,1)S(1)} %all-to-all-done.1.x_ref, bf16[2,192,3072]{2,1,0:T(8,128)(2,1)S(1)} %copy-done, bf16[2,192,3072]{2,1,0:T(8,128)(2,1)S(1)} %copy-done.1, bf16[2,192,3072]{2,1,0:T(8,128)(2,1)S(1)} %copy-done.2), custom_call_target="tpu_custom_call" | custom-call | flops 2717908992 | bytes 9437184 | tf_op jit(solution)/shard_map/pallas_call | solution.py:160
  130.2 36.2 %all_to_all.20.in_ref = bf16[16,576,128]{2,1,0:T(8,128)(2,1)S(1)} all-to-all(bf16[16,576,128]{2,1,0:T(8,128)(2,1)S(1)} %shard_map.66), channel_id=1, replica_groups=mesh['z'=32,'core'=2,'y'=4,'x'=4] {'y','x'}, dimensions={0} | all-to-all | bytes 4718592 | tf_op jit(solution)/shard_map/all_to_all | solution.py:203
  166.3 0.0 copy-start.5
  166.4 1.6 shard_map.67
  167.9 22.9 %all-to-all-start.3 = ((bf16[32,9,2,128]{3,2,1,0:T(2,128)(2,1)}), bf16[32,9,2,128]{3,2,1,0:T(2,128)(2,1)S(1)}, u32[]{:S(2)}, u32[]{:S(2)}) async-start(bf16[32,9,2,128]{3,2,1,0:T(2,128)(2,1)} %bitcast.5), calls=%async_computation.3 | async-start | bytes 294912 | tf_op jit(solution)/shard_map/all_to_all | solution.py:173
  190.9 0.1 copy.9.routes_ref
  191.0 0.0 copy-done.5
  191.0 0.1 copy.10.gates_ref
  191.0 31.7 %all-to-all-done.3 = bf16[32,9,2,128]{3,2,1,0:T(2,128)(2,1)S(1)} async-done(((bf16[32,9,2,128]{3,2,1,0:T(2,128)(2,1)}), bf16[32,9,2,128]{3,2,1,0:T(2,128)(2,1)S(1)}, u32[]{:S(2)}, u32[]{:S(2)}) %all-to-all-start.3) | async-done | bytes 147488 | tf_op jit(solution)/shard_map/all_to_all | solution.py:173
  222.8 1.4 shard_map.68
Async XLA Ops:
  6.5 1.5 copy-start.4
  6.5 1.5 copy-start.3
  6.5 74.1 %all-gather.4.cloned.1.call-start = ((), (), s32[]{:S(2)}) async-start(), calls=%async_computation.4 | async-start | bytes 3538944 | tf_op jit(solution)/shard_map/all_gather | solution.py:183
  7.3 77.7 %all-gather.6.cloned.1.call-start = ((), (), s32[]{:S(2)}) async-start(), calls=%async_computation.5 | async-start | bytes 3538944 | tf_op jit(solution)/shard_map/all_gather | solution.py:184
  9.3 61.6 %all-to-all-start = ((bf16[32,9,2,128]{3,2,1,0:T(2,128)(2,1)}), bf16[32,9,2,128]{3,2,1,0:T(2,128)(2,1)S(1)}, u32[]{:S(2)}, u32[]{:S(2)}) async-start(bf16[32,9,2,128]{3,2,1,0:T(2,128)(2,1)} %bitcast.1), calls=%async_computation | async-start | bytes 294912 | tf_op jit(solution)/shard_map/all_to_all | solution.py:173
  38.1 82.7 %all-gather.8.cloned.1.call-start = ((), (), s32[]{:S(2)}) async-start(), calls=%async_computation.6 | async-start | bytes 3538944 | tf_op jit(solution)/shard_map/all_gather | solution.py:185
  73.2 47.5 %all-to-all-start.1 = ((bf16[16,576,128]{2,1,0:T(8,128)(2,1)}), bf16[16,576,128]{2,1,0:T(8,128)(2,1)S(1)}, u32[]{:S(2)}, u32[]{:S(2)}) async-start(bf16[16,576,128]{2,1,0:T(8,128)(2,1)} %shard_map.65), calls=%async_computation.1 | async-start | bytes 4718592 | tf_op jit(solution)/shard_map/all_to_all | solution.py:191
  120.8 1.7 copy-start
  122.4 1.7 copy-start.1
  124.1 1.7 copy-start.2
  166.3 24.6 %copy-start.5 = (f32[48,4]{0,1:T(4,128)S(1)}, f32[48,4]{0,1:T(4,128)}, u32[]{:S(2)}) copy-start(f32[48,4]{0,1:T(4,128)} %param.8) | copy-start | bytes 2308
  167.9 54.8 %all-to-all-start.3 = ((bf16[32,9,2,128]{3,2,1,0:T(2,128)(2,1)}), bf16[32,9,2,128]{3,2,1,0:T(2,128)(2,1)S(1)}, u32[]{:S(2)}, u32[]{:S(2)}) async-start(bf16[32,9,2,128]{3,2,1,0:T(2,128)(2,1)} %bitcast.5), calls=%async_computation.3 | async-start | bytes 294912 | tf_op jit(solution)/shard_map/all_to_all | solution.py:173
Sparse Core Ops, SparseCore 0:
  10.0 39.0 all-gather.3
  51.8 33.0 all-gather.5
  87.6 33.0 all-gather.7

commit v2 on v1

--- a/solution.py
+++ b/solution.py
@@ -28,7 +28,7 @@
     return head, low, high
 
 
-def dispatch_kernel(slots, cap, tokens_ref, routes_ref, out_ref):
+def dispatch_kernel(slots, cap, tokens_ref, routes_ref, gates_ref, out_ref, weights_ref):
     odd = lax.rem(lax.axis_index("x"), 2) == 1
     count = tokens_ref.shape[0]
     top = routes_ref.shape[0]
@@ -45,12 +45,25 @@
     earlier = (iota((count, count), 0) < iota((count, count), 1)).astype(F32).astype(BF16)
     before = jnp.dot(named, earlier, preferred_element_type=F32)
     line_ids = iota((total, count), 0)
+    lane_ids = iota((count, total), 1)
+    diagonal = iota((count, count), 0) == iota((count, count), 1)
+
+    def column(row):
+        return jnp.sum(jnp.where(diagonal, row, 0.0), axis=1, keepdims=True)
+
     masks = [None, None, None]
+    weights = [jnp.zeros((count, total), F32) for _ in range(3)]
     for k in range(top):
-        place = jnp.sum(jnp.where(onehots[k], before, 0.0), axis=0, keepdims=True).astype(jnp.int32)
+        place = jnp.sum(jnp.where(onehots[k], before, 0.0), axis=0, keepdims=True)
+        slot_column = column(chosen[k].astype(F32)).astype(jnp.int32)
+        place_column = column(place).astype(jnp.int32)
+        gate_column = column(gates_ref[k : k + 1, :])
+        place = place.astype(jnp.int32)
         for n, line in enumerate(lines_of(chosen[k], place, cap)):
             hit = line_ids == line
             masks[n] = hit if masks[n] is None else jnp.logical_or(masks[n], hit)
+        for n, line in enumerate(lines_of(slot_column, place_column, cap)):
+            weights[n] = jnp.where(lane_ids == line, gate_column, weights[n])
     parts = (head, jnp.where(left, both, 0.0), jnp.where(left, 0.0, both))
     out = jnp.zeros((total, LANES), F32)
     for mask, part in zip(masks, parts):
@@ -58,6 +71,12 @@
             mask.astype(F32).astype(BF16), part.astype(BF16), preferred_element_type=F32
         )
     out_ref[...] = out.astype(BF16)
+    for n, weight in enumerate(weights):
+        coarse = weight.astype(BF16)
+        weights_ref[n * count : (n + 1) * count, :] = coarse
+        weights_ref[(n + 3) * count : (n + 4) * count, :] = (weight - coarse.astype(F32)).astype(
+            BF16
+        )
 
 
 def spread_kernel(cap, in_ref, out_ref):
@@ -72,7 +91,7 @@
         out_ref[n] = lines
 
 
-def ffn_kernel(x_ref, gate_ref, up_ref, down_ref, out_ref, rows_ref):
+def ffn_kernel(x_ref, gate_ref, up_ref, down_ref, other_ref, out_ref, rows_ref):
     rows = rows_ref.shape[0]
     mid = rows // 2
     left = iota((mid, LANES), 1) < HALF
@@ -90,15 +109,15 @@
         rows_ref[mid:, start + LANES : start + 2 * LANES] = lower.astype(BF16)
     hidden = []
     last = (((1,), (1,)), ((), ()))
-    for h in range(2):
-        gate = lax.dot_general(rows_ref[...], gate_ref[h], last, preferred_element_type=F32)
-        up = lax.dot_general(rows_ref[...], up_ref[h], last, preferred_element_type=F32)
+    for gates, ups in ((gate_ref[0], up_ref[0]), (other_ref[0], other_ref[1])):
+        gate = lax.dot_general(rows_ref[...], gates, last, preferred_element_type=F32)
+        up = lax.dot_general(rows_ref[...], ups, last, preferred_element_type=F32)
         hidden.append((gate / (1.0 + jnp.exp(-gate)) * up).astype(BF16))
     for n in range(pairs):
         start = n * wide
         out = jnp.dot(hidden[0], down_ref[0, :, start : start + wide], preferred_element_type=F32)
         out = out + jnp.dot(
-            hidden[1], down_ref[1, :, start : start + wide], preferred_element_type=F32
+            hidden[1], other_ref[2, :, start : start + wide], preferred_element_type=F32
         )
         out_ref[2 * n, :rows, :] = out[:, :LANES].astype(BF16)
         out_ref[2 * n + 1, :rows, :] = out[:, 2 * LANES :].astype(BF16)
@@ -122,50 +141,32 @@
     out_ref[...] = jnp.dot(order, acc.astype(BF16), preferred_element_type=F32).astype(BF16)
 
 
-def combine_kernel(slots, cap, in_ref, routes_ref, gates_ref, out_ref):
+def combine_kernel(in_ref, weights_ref, out_ref):
     odd = lax.rem(lax.axis_index("x"), 2) == 1
-    count, top = routes_ref.shape
-    total = in_ref.shape[0]
-    slot_ids = iota((count, slots), 1)
-    chosen = [routes_ref[:, k : k + 1] for k in range(top)]
-    onehots = [chosen[k] == slot_ids for k in range(top)]
-    named = functools.reduce(jnp.logical_or, onehots).astype(F32).astype(BF16)
-    earlier = (iota((count, count), 0) > iota((count, count), 1)).astype(F32).astype(BF16)
-    before = jnp.dot(earlier, named, preferred_element_type=F32)
-    line_ids = iota((count, total), 1)
-    weights = [jnp.zeros((count, total), F32) for _ in range(3)]
-    for k in range(top):
-        place = jnp.sum(jnp.where(onehots[k], before, 0.0), axis=1, keepdims=True).astype(jnp.int32)
-        for n, line in enumerate(lines_of(chosen[k], place, cap)):
-            weights[n] = jnp.where(line_ids == line, gates_ref[:, k : k + 1], weights[n])
-    lines = in_ref[...]
-    sums = []
-    for weight in weights:
-        coarse = weight.astype(BF16)
-        fine = (weight - coarse.astype(F32)).astype(BF16)
-        sums.append(
-            jnp.dot(coarse, lines, preferred_element_type=F32)
-            + jnp.dot(fine, lines, preferred_element_type=F32)
-        )
-    head, tail = sums[0], sums[1][:, :HALF] + sums[2][:, HALF:]
+    count = out_ref.shape[0]
+    sums = jnp.dot(weights_ref[...], in_ref[...], preferred_element_type=F32)
+    sums = sums[: 3 * count] + sums[3 * count :]
+    head = sums[:count]
+    tail = sums[count : 2 * count, :HALF] + sums[2 * count :, HALF:]
     out = jnp.where(
         odd, jnp.concatenate([tail, head], axis=1), jnp.concatenate([head, tail], axis=1)
     )
     out_ref[...] = out.astype(BF16)
 
 
-def call(kernel, shape, *args, scratch=(), limit=16, flops=0):
+def call(kernel, shapes, *args, scratch=(), limit=16, flops=0):
     vmem = pl.BlockSpec(memory_space=pltpu.VMEM)
     size = sum(a.size * a.dtype.itemsize for a in args)
-    return pl.pallas_call(
+    outs = pl.pallas_call(
         kernel,
-        out_shape=jax.ShapeDtypeStruct(shape, BF16),
+        out_shape=[jax.ShapeDtypeStruct(shape, BF16) for shape in shapes],
         in_specs=[vmem] * len(args),
-        out_specs=vmem,
+        out_specs=[vmem] * len(shapes),
         scratch_shapes=list(scratch),
         compiler_params=pltpu.CompilerParams(vmem_limit_bytes=limit * 1024 * 1024),
         cost_estimate=pl.CostEstimate(flops=flops, bytes_accessed=size, transcendentals=0),
     )(*args)
+    return outs if len(shapes) > 1 else outs[0]
 
 
 def exchange_z(lines, slots):
@@ -180,32 +181,32 @@
     cap = min(count, 2 * count * top // slots)
     total = slots * cap * 3 // 2
     rows = slots * cap
-    gate_all = lax.all_gather(w_gate.swapaxes(1, 2), "core", axis=0, tiled=True)
-    up_all = lax.all_gather(w_up.swapaxes(1, 2), "core", axis=0, tiled=True)
-    down_all = lax.all_gather(w_down, "core", axis=0, tiled=True)
-    outgoing = call(
-        functools.partial(dispatch_kernel, slots, cap), (total, LANES), tokens, routes.T
+    own = [w_gate.swapaxes(1, 2), w_up.swapaxes(1, 2), w_down]
+    other = lax.ppermute(jnp.concatenate(own, axis=0), "core", [(0, 1), (1, 0)])
+    outgoing, weights = call(
+        functools.partial(dispatch_kernel, slots, cap),
+        [(total, LANES), (6 * count, total)],
+        tokens,
+        routes.T,
+        gates.T,
     )
     incoming = exchange_z(outgoing, slots)
-    copies = call(functools.partial(spread_kernel, cap), (shares, total, LANES), incoming)
+    copies = call(functools.partial(spread_kernel, cap), [(shares, total, LANES)], incoming)
     features = lax.all_to_all(copies, ("y", "x"), split_axis=0, concat_axis=0, tiled=True)
     partials = call(
         ffn_kernel,
-        (shares, total, LANES),
+        [(shares, total, LANES)],
         features,
-        gate_all,
-        up_all,
-        down_all,
+        *own,
+        other,
         scratch=[pltpu.VMEM((rows, shares * SHARE), BF16)],
-        limit=40,
+        limit=32,
         flops=2 * rows * shares * SHARE * 6 * SHARE,
     )
     landed = lax.all_to_all(partials, ("y", "x"), split_axis=0, concat_axis=0, tiled=True)
-    summed = call(functools.partial(sum_kernel, cap), (total, LANES), landed)
+    summed = call(functools.partial(sum_kernel, cap), [(total, LANES)], landed)
     returned = exchange_z(summed, slots)
-    return call(
-        functools.partial(combine_kernel, slots, cap), (count, SHARE), returned, routes, gates
-    )
+    return call(combine_kernel, [(count, SHARE)], returned, weights)
 
 
 def split_mesh(mesh):

time: 232 us -> 178 us (0.77)
  blocking collectives: 36.2 us -> 164 us
  waiting for transfers between devices: 106 us -> 0.01 us
  starting transfers between devices: 59.1 us -> 1.92 us
  between operations: 13.2 us -> 0.11 us
  local copies, waits for them, and re-layouts: 5.19 us -> 0.03 us
  Pallas kernels: 11 us -> 8.08 us
    all_to_all x0 -> x3, blocking collectives: none -> 132 us  [the longest x2 96.6 us: exchange_z(): lax.all_to_all(blocks, 'z', split_axis=0, concat_axis=0, tiled=True)]
    all_to_all x3 -> x0, waiting for transfers between devices: 63.8 us -> none  [the longest x2 63.8 us: exchange_z(): lax.all_to_all(blocks, 'z', split_axis=0, concat_axis=0, tiled=True)]
    all_to_all x3 -> x0, starting transfers between devices: 59.1 us -> none  [the longest x2 51.6 us: exchange_z(): lax.all_to_all(blocks, 'z', split_axis=0, concat_axis=0, tiled=True)]
    all_gather x3 -> x0, waiting for transfers between devices: 40.1 us -> none  [the longest x1 35.8 us: per_device(): down_all = lax.all_gather(w_down, 'core', axis=0, tiled=True)]
    unnamed x14 -> x12, local copies, waits for them, and re-layouts: 5.19 us -> 0.03 us
    all_to_all x1, blocking collectives: 36.2 us -> 32 us  [per_device(): lax.all_to_all(partials, ('y', 'x'), split_axis=0, concat_axis=0, tiled=T...]
    pallas_call x5, Pallas kernels: 11 us -> 8.08 us  [call(): pl.pallas_call(kernel, out_shape=[jax.ShapeDtypeStruct(shape, BF16) for s...]
  transfers between devices with their start and end apart: 6 -> 1, of which waited for: 4 -> 0; matrix products, arithmetic and copies ran while one was open for 0% -> 0% of each run, Pallas kernels for 2% -> 1%
where the time goes in v2:
time: 178 us; the launch traced here: 176 us
  blocking collectives  164 us (92%)
  Pallas kernels  8.08 us (5%)
  other arithmetic  2.2 us (1%)
  starting transfers between devices  1.92 us (1%)
    all_to_all x2, blocking collectives, exchange_z(): lax.all_to_all(blocks, 'z', split_axis=0, concat_axis=0, tiled=True)  96.6 us
    all_to_all x1, blocking collectives, per_device(): lax.all_to_all(copies, ('y', 'x'), split_axis=0, concat_axis=0, tiled=True)  35.4 us
    all_to_all x1, blocking collectives, per_device(): lax.all_to_all(partials, ('y', 'x'), split_axis=0, concat_axis=0, tiled=T...  32 us
    pallas_call x5, Pallas kernels, call(): pl.pallas_call(kernel, out_shape=[jax.ShapeDtypeStruct(shape, BF16) for s...  8.08 us
  transfers between devices with their start and end apart: 1, of which 0 were waited for; matrix products, arithmetic and copies ran while one was open for 0% of the time, Pallas kernels for 1%

profile of v2, /device:TPU:6, one launch (start us, length us, event | category | flops | bytes accessed | tf_op | source)
XLA Modules:
  0.0 176.4 jit_solution(17866099063663537179)
XLA Ops:
  0.0 0.0 copy-start.3
  0.0 0.0 copy-start.4
  0.0 0.0 copy-start.5
  0.0 2.2 %pad_maximum_fusion = bf16[3,192,3072]{2,1,0:T(8,128)(2,1)S(1)} fusion(bf16[1,192,3072]{2,1,0:T(8,128)(2,1)} %down_ref.1, bf16[1,192,3072]{2,1,0:T(8,128)(2,1)} %bitcast.10, bf16[1,192,3072]{2,1,0:T(8,128)(2,1)} %bitcast.8), kind=kLoop, calls=%fused_computation | loop fusion | flops 3538944 | bytes 7077888 | tf_op jit(solution)/shard_map/concatenate | solution.py:185
  2.2 1.9 %collective-permute-start = (bf16[3,192,3072]{2,1,0:T(8,128)(2,1)S(1)}, bf16[3,192,3072]{2,1,0:T(8,128)(2,1)S(1)}, u32[]{:S(2)}, u32[]{:S(2)}) collective-permute-start(bf16[3,192,3072]{2,1,0:T(8,128)(2,1)S(1)} %pad_maximum_fusion), channel_id=1, source_target_pairs={{0,16},{16,0},{1,17},{17,1},{2,18},{18,2},{3,19},{19,3},{4,20},{20... | collective-permute-start | bytes 10616840 | tf_op jit(solution)/shard_map/ppermute | solution.py:185
  4.1 0.0 copy-done.3
  4.2 0.0 copy-done.4
  4.2 0.0 copy-done.5
  4.2 1.0 shard_map.64
  5.2 62.1 %all_to_all.20 = bf16[32,9,2,128]{3,2,1,0:T(2,128)(2,1)S(1)} all-to-all(bf16[32,9,2,128]{3,2,1,0:T(2,128)(2,1)S(1)} %bitcast.15), channel_id=1, replica_groups=mesh['z'=32,'core'=2,'y'=4,'x'=4] {'z'}, dimensions={0} | all-to-all | bytes 294912 | tf_op jit(solution)/shard_map/all_to_all | solution.py:174
  67.2 0.8 shard_map.65
  68.0 0.0 copy-start
  68.0 0.0 copy-start.1
  68.0 0.0 copy-start.2
  68.1 35.4 %all_to_all.21.x_ref = bf16[16,576,128]{2,1,0:T(8,128)(2,1)S(1)} all-to-all(bf16[16,576,128]{2,1,0:T(8,128)(2,1)S(1)} %shard_map.65), channel_id=1, replica_groups=mesh['z'=32,'core'=2,'y'=4,'x'=4] {'y','x'}, dimensions={0} | all-to-all | bytes 4718592 | tf_op jit(solution)/shard_map/all_to_all | solution.py:195
  103.5 0.0 collective-permute-done.other_ref
  103.5 0.0 copy-done
  103.5 0.0 copy-done.1
  103.5 0.0 copy-done.2
  103.5 4.4 %shard_map.66 = bf16[16,576,128]{2,1,0:T(8,128)(2,1)S(1)} custom-call(bf16[16,576,128]{2,1,0:T(8,128)(2,1)S(1)} %all_to_all.21.x_ref, bf16[1,192,3072]{2,1,0:T(8,128)(2,1)S(1)} %bitcast.9, bf16[1,192,3072]{2,1,0:T(8,128)(2,1)S(1)} %bitcast.11, bf16[1,192,3072]{2,1,0:T(8,128)(2,1)S(1)} %copy-done.2, bf16[3,192,3072]{2,1,0:T(8,128)(2,1)S(1)} %collective-permute-done.other_ref), custom_call_target="tpu_custom_call" | custom-call | flops 2717908992 | bytes 9437184 | tf_op jit(solution)/shard_map/pallas_call | solution.py:160
  107.9 32.0 %all_to_all.22.in_ref = bf16[16,576,128]{2,1,0:T(8,128)(2,1)S(1)} all-to-all(bf16[16,576,128]{2,1,0:T(8,128)(2,1)S(1)} %shard_map.66), channel_id=1, replica_groups=mesh['z'=32,'core'=2,'y'=4,'x'=4] {'y','x'}, dimensions={0} | all-to-all | bytes 4718592 | tf_op jit(solution)/shard_map/all_to_all | solution.py:206
  140.0 0.9 shard_map.67
  140.9 34.5 %all_to_all.23 = bf16[32,9,2,128]{3,2,1,0:T(2,128)(2,1)S(1)} all-to-all(bf16[32,9,2,128]{3,2,1,0:T(2,128)(2,1)S(1)} %bitcast.13), channel_id=1, replica_groups=mesh['z'=32,'core'=2,'y'=4,'x'=4] {'z'}, dimensions={0} | all-to-all | bytes 294912 | tf_op jit(solution)/shard_map/all_to_all | solution.py:174
  175.4 0.9 shard_map.68
Async XLA Ops:
  0.0 4.1 %copy-start.3 = (bf16[48,192]{1,0:T(8,128)(2,1)S(1)}, bf16[48,192]{1,0:T(8,128)(2,1)}, u32[]{:S(2)}) copy-start(bf16[48,192]{1,0:T(8,128)(2,1)} %tokens_ref.1) | copy-start | bytes 55300
  0.0 4.2 %copy-start.4 = (s32[48,4]{0,1:T(4,128)S(1)}, s32[48,4]{0,1:T(4,128)}, u32[]{:S(2)}) copy-start(s32[48,4]{0,1:T(4,128)} %param.7) | copy-start | bytes 2308
  0.0 4.2 %copy-start.5 = (f32[48,4]{0,1:T(4,128)S(1)}, f32[48,4]{0,1:T(4,128)}, u32[]{:S(2)}) copy-start(f32[48,4]{0,1:T(4,128)} %param.8) | copy-start | bytes 2308
  2.2 101.3 %collective-permute-start = (bf16[3,192,3072]{2,1,0:T(8,128)(2,1)S(1)}, bf16[3,192,3072]{2,1,0:T(8,128)(2,1)S(1)}, u32[]{:S(2)}, u32[]{:S(2)}) collective-permute-start(bf16[3,192,3072]{2,1,0:T(8,128)(2,1)S(1)} %pad_maximum_fusion), channel_id=1, source_target_pairs={{0,16},{16,0},{1,17},{17,1},{2,18},{18,2},{3,19},{19,3},{4,20},{20... | collective-permute-start | bytes 10616840 | tf_op jit(solution)/shard_map/ppermute | solution.py:185
  68.0 35.5 %copy-start = (bf16[1,3072,192]{1,2,0:T(8,128)(2,1)S(1)}, bf16[1,3072,192]{1,2,0:T(8,128)(2,1)}, u32[]{:S(2)}) copy-start(bf16[1,3072,192]{1,2,0:T(8,128)(2,1)} %param.9) | copy-start | bytes 3538948
  68.0 35.5 %copy-start.1 = (bf16[1,3072,192]{1,2,0:T(8,128)(2,1)S(1)}, bf16[1,3072,192]{1,2,0:T(8,128)(2,1)}, u32[]{:S(2)}) copy-start(bf16[1,3072,192]{1,2,0:T(8,128)(2,1)} %param.10) | copy-start | bytes 3538948
  68.0 35.5 %copy-start.2 = (bf16[1,192,3072]{2,1,0:T(8,128)(2,1)S(1)}, bf16[1,192,3072]{2,1,0:T(8,128)(2,1)}, u32[]{:S(2)}) copy-start(bf16[1,192,3072]{2,1,0:T(8,128)(2,1)} %down_ref.1) | copy-start | bytes 3538948

commit v3 on v2

--- a/solution.py
+++ b/solution.py
@@ -28,7 +28,26 @@
     return head, low, high
 
 
-def dispatch_kernel(slots, cap, tokens_ref, routes_ref, gates_ref, out_ref, weights_ref):
+def dispatch_kernel(
+    slots,
+    cap,
+    tokens_ref,
+    routes_ref,
+    gates_ref,
+    w_gate_ref,
+    w_up_ref,
+    w_down_ref,
+    out_ref,
+    weights_ref,
+    own_ref,
+    sems,
+):
+    copies = [
+        pltpu.make_async_copy(ref.at[0], own_ref.at[n], sems.at[n])
+        for n, ref in enumerate((w_gate_ref, w_up_ref, w_down_ref))
+    ]
+    for copy in copies:
+        copy.start()
     odd = lax.rem(lax.axis_index("x"), 2) == 1
     count = tokens_ref.shape[0]
     top = routes_ref.shape[0]
@@ -77,45 +96,56 @@
         weights_ref[(n + 3) * count : (n + 4) * count, :] = (weight - coarse.astype(F32)).astype(
             BF16
         )
+    for copy in copies:
+        copy.wait()
 
 
 def spread_kernel(cap, in_ref, out_ref):
-    total = in_ref.shape[0]
-    half, group = cap // 2, in_ref.shape[0] // 3
+    total = in_ref.shape[1]
+    half, group = cap // 2, total // 3
     place = iota((total, 1), 0)
     kind, rest = place // group, place % group
     source = rest // half * (3 * half) + rest % half + kind * half
     order = (source == iota((total, total), 1)).astype(F32).astype(BF16)
-    lines = jnp.dot(order, in_ref[...], preferred_element_type=F32).astype(BF16)
-    for n in range(out_ref.shape[0]):
-        out_ref[n] = lines
-
-
-def ffn_kernel(x_ref, gate_ref, up_ref, down_ref, other_ref, out_ref, rows_ref):
+    for share in range(in_ref.shape[0]):
+        lines = jnp.dot(order, in_ref[share], preferred_element_type=F32).astype(BF16)
+        for n in range(out_ref.shape[0]):
+            out_ref[n, share] = lines
+
+
+def ffn_kernel(x_ref, own_ref, other_ref, out_ref, rows_ref):
+    side = x_ref.shape[0]
+    first = lax.axis_index("core") == 0
+
+    def block(n):
+        y, x = n // side, n % side
+        return jnp.where(first, y, x), jnp.where(first, x, y)
+
     rows = rows_ref.shape[0]
     mid = rows // 2
     left = iota((mid, LANES), 1) < HALF
-    pairs = x_ref.shape[0] // 2
+    pairs = out_ref.shape[0] // 2
     wide = 3 * LANES
     for n in range(pairs):
         start = n * wide
-        rows_ref[:, start : start + LANES] = x_ref[2 * n, :rows, :]
-        rows_ref[:, start + 2 * LANES : start + wide] = x_ref[2 * n + 1, :rows, :]
-        a = x_ref[2 * n, rows:, :].astype(F32)
-        b = x_ref[2 * n + 1, rows:, :].astype(F32)
+        even, odd = block(2 * n), block(2 * n + 1)
+        rows_ref[:, start : start + LANES] = x_ref[even[0], even[1], :rows, :]
+        rows_ref[:, start + 2 * LANES : start + wide] = x_ref[odd[0], odd[1], :rows, :]
+        a = x_ref[even[0], even[1], rows:, :].astype(F32)
+        b = x_ref[odd[0], odd[1], rows:, :].astype(F32)
         upper = jnp.where(left, a, pltpu.roll(b, HALF, 1))
         lower = jnp.where(left, pltpu.roll(a, HALF, 1), b)
         rows_ref[:mid, start + LANES : start + 2 * LANES] = upper.astype(BF16)
         rows_ref[mid:, start + LANES : start + 2 * LANES] = lower.astype(BF16)
     hidden = []
     last = (((1,), (1,)), ((), ()))
-    for gates, ups in ((gate_ref[0], up_ref[0]), (other_ref[0], other_ref[1])):
+    for gates, ups in ((own_ref[0], own_ref[1]), (other_ref[0], other_ref[1])):
         gate = lax.dot_general(rows_ref[...], gates, last, preferred_element_type=F32)
         up = lax.dot_general(rows_ref[...], ups, last, preferred_element_type=F32)
         hidden.append((gate / (1.0 + jnp.exp(-gate)) * up).astype(BF16))
     for n in range(pairs):
         start = n * wide
-        out = jnp.dot(hidden[0], down_ref[0, :, start : start + wide], preferred_element_type=F32)
+        out = jnp.dot(hidden[0], own_ref[2, :, start : start + wide], preferred_element_type=F32)
         out = out + jnp.dot(
             hidden[1], other_ref[2, :, start : start + wide], preferred_element_type=F32
         )
@@ -154,18 +184,18 @@
     out_ref[...] = out.astype(BF16)
 
 
-def call(kernel, shapes, *args, scratch=(), limit=16, flops=0):
+def call(kernel, shapes, *args, hbm=(), scratch=(), limit=16, flops=0, keep=False):
     vmem = pl.BlockSpec(memory_space=pltpu.VMEM)
-    size = sum(a.size * a.dtype.itemsize for a in args)
+    size = sum(a.size * a.dtype.itemsize for a in (*args, *hbm))
     outs = pl.pallas_call(
         kernel,
-        out_shape=[jax.ShapeDtypeStruct(shape, BF16) for shape in shapes],
-        in_specs=[vmem] * len(args),
+        out_shape=[(pltpu.VMEM if keep else jax.ShapeDtypeStruct)(shape, BF16) for shape in shapes],
+        in_specs=[vmem] * len(args) + [pl.BlockSpec(memory_space=pltpu.HBM)] * len(hbm),
         out_specs=[vmem] * len(shapes),
         scratch_shapes=list(scratch),
         compiler_params=pltpu.CompilerParams(vmem_limit_bytes=limit * 1024 * 1024),
         cost_estimate=pl.CostEstimate(flops=flops, bytes_accessed=size, transcendentals=0),
-    )(*args)
+    )(*args, *hbm)
     return outs if len(shapes) > 1 else outs[0]
 
 
@@ -175,29 +205,43 @@
 
 
 def per_device(tokens, routes, gates, w_gate, w_up, w_down):
-    slots = lax.axis_size("z")
-    shares = lax.axis_size("y") * lax.axis_size("x")
+    slots, side = lax.axis_size("z"), lax.axis_size("x")
+    shares = lax.axis_size("y") * side
     count, top = routes.shape
     cap = min(count, 2 * count * top // slots)
     total = slots * cap * 3 // 2
     rows = slots * cap
-    own = [w_gate.swapaxes(1, 2), w_up.swapaxes(1, 2), w_down]
-    other = lax.ppermute(jnp.concatenate(own, axis=0), "core", [(0, 1), (1, 0)])
-    outgoing, weights = call(
+    plane = ("core", "y", "x")
+    along = range(side)
+    along_x = [[[c * shares + y * side + x for x in along] for y in along] for c in range(2)]
+    along_y = [[[c * shares + y * side + x for y in along] for x in along] for c in range(2)]
+    short = along_x[0] + along_y[1]
+    long = along_y[0] + along_x[1]
+    outgoing, weights, own = call(
         functools.partial(dispatch_kernel, slots, cap),
-        [(total, LANES), (6 * count, total)],
+        [(total, LANES), (6 * count, total), (3, *w_down.shape[1:])],
         tokens,
         routes.T,
         gates.T,
-    )
+        hbm=(w_gate.swapaxes(1, 2), w_up.swapaxes(1, 2), w_down),
+        scratch=[pltpu.SemaphoreType.DMA((3,))],
+        limit=54,
+        keep=True,
+    )
+    other = lax.ppermute(own, "core", [(0, 1), (1, 0)])
     incoming = exchange_z(outgoing, slots)
-    copies = call(functools.partial(spread_kernel, cap), [(shares, total, LANES)], incoming)
-    features = lax.all_to_all(copies, ("y", "x"), split_axis=0, concat_axis=0, tiled=True)
+    line = lax.all_gather(incoming, plane, axis_index_groups=short)
+    copies = call(
+        functools.partial(spread_kernel, cap), [(side, side, total, LANES)], line, limit=24
+    )
+    features = lax.all_to_all(
+        copies, plane, split_axis=0, concat_axis=0, axis_index_groups=long, tiled=True
+    )
     partials = call(
         ffn_kernel,
         [(shares, total, LANES)],
         features,
-        *own,
+        own,
         other,
         scratch=[pltpu.VMEM((rows, shares * SHARE), BF16)],
         limit=32,

time: 178 us -> 171 us (0.961)
  blocking collectives: 164 us -> 157 us
  Pallas kernels: 8.08 us -> 10.4 us
  other arithmetic: 2.2 us -> 0 us
    all_to_all x1, blocking collectives: 35.4 us -> 22.2 us  [per_device(): lax.all_to_all(copies, plane, split_axis=0, concat_axis=0, axis_index_gro...]
    all_gather x0 -> x1, blocking collectives: none -> 12.9 us  [per_device(): line = lax.all_gather(incoming, plane, axis_index_groups=short)]
    all_to_all x2, blocking collectives: 96.6 us -> 92.7 us  [exchange_z(): lax.all_to_all(blocks, 'z', split_axis=0, concat_axis=0, tiled=True)]
    all_to_all x1, blocking collectives: 32 us -> 29 us  [per_device(): lax.all_to_all(partials, ('y', 'x'), split_axis=0, concat_axis=0, tiled=T...]
    pallas_call x5, Pallas kernels: 8.08 us -> 10.4 us  [call(): pl.pallas_call(kernel, out_shape=[(pltpu.VMEM if keep else jax.ShapeDtype...]
    concatenate x1 -> x0, other arithmetic: 2.2 us -> none  [per_device(): other = lax.ppermute(jnp.concatenate(own, axis=0), 'core', [(0, 1), (1, 0)])]
where the time goes in v3:
time: 171 us; the launch traced here: 169 us
  blocking collectives  157 us (92%)
  Pallas kernels  10.4 us (6%)
  starting transfers between devices  1.92 us (1%)
    all_to_all x2, blocking collectives, exchange_z(): lax.all_to_all(blocks, 'z', split_axis=0, concat_axis=0, tiled=True)  92.7 us
    all_to_all x1, blocking collectives, per_device(): lax.all_to_all(partials, ('y', 'x'), split_axis=0, concat_axis=0, tiled=T...  29 us
    all_to_all x1, blocking collectives, per_device(): lax.all_to_all(copies, plane, split_axis=0, concat_axis=0, axis_index_gro...  22.2 us
    all_gather x1, blocking collectives, per_device(): line = lax.all_gather(incoming, plane, axis_index_groups=short)  12.9 us
    pallas_call x5, Pallas kernels, call(): pl.pallas_call(kernel, out_shape=[(pltpu.VMEM if keep else jax.ShapeDtype...  10.4 us
  transfers between devices with their start and end apart: 1, of which 0 were waited for; matrix products, arithmetic and copies ran while one was open for 0% of the time, Pallas kernels for 1%

profile of v3, /device:TPU:6, one launch (start us, length us, event | category | flops | bytes accessed | tf_op | source)
XLA Modules:
  0.0 169.1 jit_solution(14664519041309851843)
XLA Ops:
  0.0 2.8 %shard_map.64 = (bf16[576,128]{1,0:T(8,128)(2,1)S(1)}, bf16[288,576]{1,0:T(8,128)(2,1)S(1)}, bf16[3,192,3072]{2,1,0:T(8,128)(2,1)S(1)}) custom-call(bf16[48,192]{1,0:T(8,128)(2,1)} %tokens_ref.1, s32[4,48]{1,0:T(4,128)} %bitcast.14, f32[4,48]{1,0:T(4,128)} %bitcast.15, bf16[1,192,3072]{2,1,0:T(8,128)(2,1)} %bitcast.11, bf16[1,192,3072]{2,1,0:T(8,128)(2,1)} %bitcast.12, ...), custom_call_target="tpu_custom_call" | custom-call | bytes 3558912 | tf_op jit(solution)/shard_map/pallas_call | solution.py:190
  2.8 1.9 %collective-permute-start = (bf16[3,192,3072]{2,1,0:T(8,128)(2,1)S(1)}, bf16[3,192,3072]{2,1,0:T(8,128)(2,1)S(1)}, u32[]{:S(2)}, u32[]{:S(2)}) collective-permute-start(bf16[3,192,3072]{2,1,0:T(8,128)(2,1)S(1)} %get-tuple-element.9.own_ref), channel_id=1, source_target_pairs={{0,16},{16,0},{1,17},{17,1},{2,18},{18,2},{3,19},{19,3},{4,20},{20... | collective-permute-start | bytes 10616840 | tf_op jit(solution)/shard_map/ppermute | solution.py:231
  4.7 62.1 %all_to_all.20 = bf16[32,9,2,128]{3,2,1,0:T(2,128)(2,1)S(1)} all-to-all(bf16[32,9,2,128]{3,2,1,0:T(2,128)(2,1)S(1)} %bitcast.10), channel_id=1, replica_groups=mesh['z'=32,'core'=2,'y'=4,'x'=4] {'z'}, dimensions={0} | all-to-all | bytes 294912 | tf_op jit(solution)/shard_map/all_to_all | solution.py:204
  66.8 12.9 %all_gather.3.in_ref = bf16[4,576,128]{2,1,0:T(8,128)(2,1)S(1)} all-gather(bf16[1,576,128]{2,1,0:T(8,128)(2,1)S(1)} %bitcast.13), channel_id=1, replica_groups={{0,1,2,3},{4,5,6,7},{8,9,10,11},{12,13,14,15},{16,20,24,28},{17,21,25,2..., dimensions={0}, use_global_device_ids=true | all-gather | bytes 737280 | tf_op jit(solution)/shard_map/all_gather | solution.py:233
  79.7 1.3 shard_map.65
  81.0 22.2 %all_to_all.21.x_ref = bf16[4,4,576,128]{3,2,1,0:T(8,128)(2,1)S(1)} all-to-all(bf16[4,4,576,128]{3,2,1,0:T(8,128)(2,1)S(1)} %shard_map.65), channel_id=1, replica_groups={{0,4,8,12},{1,5,9,13},{2,6,10,14},{3,7,11,15},{16,17,18,19},{20,21,22,2..., dimensions={0} | all-to-all | bytes 4718592 | tf_op jit(solution)/shard_map/all_to_all | solution.py:237
  103.1 0.0 collective-permute-done.other_ref
  103.1 4.5 %shard_map.66 = bf16[16,576,128]{2,1,0:T(8,128)(2,1)S(1)} custom-call(bf16[4,4,576,128]{3,2,1,0:T(8,128)(2,1)S(1)} %all_to_all.21.x_ref, bf16[3,192,3072]{2,1,0:T(8,128)(2,1)S(1)} %get-tuple-element.9.own_ref, bf16[3,192,3072]{2,1,0:T(8,128)(2,1)S(1)} %collective-permute-done.other_ref), custom_call_target="tpu_custom_call" | custom-call | flops 2717908992 | bytes 9437184 | tf_op jit(solution)/shard_map/pallas_call | solution.py:190
  107.6 29.0 %all_to_all.22.in_ref = bf16[16,576,128]{2,1,0:T(8,128)(2,1)S(1)} all-to-all(bf16[16,576,128]{2,1,0:T(8,128)(2,1)S(1)} %shard_map.66), channel_id=1, replica_groups=mesh['z'=32,'core'=2,'y'=4,'x'=4] {'y','x'}, dimensions={0} | all-to-all | bytes 4718592 | tf_op jit(solution)/shard_map/all_to_all | solution.py:250
  136.6 0.9 shard_map.67
  137.5 30.7 %all_to_all.23 = bf16[32,9,2,128]{3,2,1,0:T(2,128)(2,1)S(1)} all-to-all(bf16[32,9,2,128]{3,2,1,0:T(2,128)(2,1)S(1)} %bitcast.8), channel_id=1, replica_groups=mesh['z'=32,'core'=2,'y'=4,'x'=4] {'z'}, dimensions={0} | all-to-all | bytes 294912 | tf_op jit(solution)/shard_map/all_to_all | solution.py:204
  168.2 0.9 shard_map.68
Async XLA Ops:
  2.8 100.4 %collective-permute-start = (bf16[3,192,3072]{2,1,0:T(8,128)(2,1)S(1)}, bf16[3,192,3072]{2,1,0:T(8,128)(2,1)S(1)}, u32[]{:S(2)}, u32[]{:S(2)}) collective-permute-start(bf16[3,192,3072]{2,1,0:T(8,128)(2,1)S(1)} %get-tuple-element.9.own_ref), channel_id=1, source_target_pairs={{0,16},{16,0},{1,17},{17,1},{2,18},{18,2},{3,19},{19,3},{4,20},{20... | collective-permute-start | bytes 10616840 | tf_op jit(solution)/shard_map/ppermute | solution.py:231

commit v4 on v3

--- a/solution.py
+++ b/solution.py
@@ -113,14 +113,9 @@
             out_ref[n, share] = lines
 
 
-def ffn_kernel(x_ref, own_ref, other_ref, out_ref, rows_ref):
-    side = x_ref.shape[0]
-    first = lax.axis_index("core") == 0
-
-    def block(n):
-        y, x = n // side, n % side
-        return jnp.where(first, y, x), jnp.where(first, x, y)
-
+def ffn_kernel(x_ref, own_ref, other_hbm, out_ref, rows_ref, other_ref, sem):
+    copy = pltpu.make_async_copy(other_hbm, other_ref, sem)
+    copy.start()
     rows = rows_ref.shape[0]
     mid = rows // 2
     left = iota((mid, LANES), 1) < HALF
@@ -128,20 +123,21 @@
     wide = 3 * LANES
     for n in range(pairs):
         start = n * wide
-        even, odd = block(2 * n), block(2 * n + 1)
-        rows_ref[:, start : start + LANES] = x_ref[even[0], even[1], :rows, :]
-        rows_ref[:, start + 2 * LANES : start + wide] = x_ref[odd[0], odd[1], :rows, :]
-        a = x_ref[even[0], even[1], rows:, :].astype(F32)
-        b = x_ref[odd[0], odd[1], rows:, :].astype(F32)
+        rows_ref[:, start : start + LANES] = x_ref[2 * n, :rows, :]
+        rows_ref[:, start + 2 * LANES : start + wide] = x_ref[2 * n + 1, :rows, :]
+        a = x_ref[2 * n, rows:, :].astype(F32)
+        b = x_ref[2 * n + 1, rows:, :].astype(F32)
         upper = jnp.where(left, a, pltpu.roll(b, HALF, 1))
         lower = jnp.where(left, pltpu.roll(a, HALF, 1), b)
         rows_ref[:mid, start + LANES : start + 2 * LANES] = upper.astype(BF16)
         rows_ref[mid:, start + LANES : start + 2 * LANES] = lower.astype(BF16)
     hidden = []
     last = (((1,), (1,)), ((), ()))
-    for gates, ups in ((own_ref[0], own_ref[1]), (other_ref[0], other_ref[1])):
-        gate = lax.dot_general(rows_ref[...], gates, last, preferred_element_type=F32)
-        up = lax.dot_general(rows_ref[...], ups, last, preferred_element_type=F32)
+    for ref in (own_ref, other_ref):
+        if ref is other_ref:
+            copy.wait()
+        gate = lax.dot_general(rows_ref[...], ref[0], last, preferred_element_type=F32)
+        up = lax.dot_general(rows_ref[...], ref[1], last, preferred_element_type=F32)
         hidden.append((gate / (1.0 + jnp.exp(-gate)) * up).astype(BF16))
     for n in range(pairs):
         start = n * wide
@@ -184,12 +180,15 @@
     out_ref[...] = out.astype(BF16)
 
 
-def call(kernel, shapes, *args, hbm=(), scratch=(), limit=16, flops=0, keep=False):
+def call(kernel, shapes, *args, hbm=(), scratch=(), limit=16, flops=0, keep=None):
     vmem = pl.BlockSpec(memory_space=pltpu.VMEM)
     size = sum(a.size * a.dtype.itemsize for a in (*args, *hbm))
     outs = pl.pallas_call(
         kernel,
-        out_shape=[(pltpu.VMEM if keep else jax.ShapeDtypeStruct)(shape, BF16) for shape in shapes],
+        out_shape=[
+            (pltpu.VMEM if n == keep else jax.ShapeDtypeStruct)(shape, BF16)
+            for n, shape in enumerate(shapes)
+        ],
         in_specs=[vmem] * len(args) + [pl.BlockSpec(memory_space=pltpu.HBM)] * len(hbm),
         out_specs=[vmem] * len(shapes),
         scratch_shapes=list(scratch),
@@ -204,19 +203,31 @@
     return lax.all_to_all(blocks, "z", split_axis=0, concat_axis=0, tiled=True).reshape(lines.shape)
 
 
+def spread(cap, lines, copies):
+    shape = (copies, *lines.shape)
+    return call(functools.partial(spread_kernel, cap), [shape], lines, limit=24)
+
+
+def gather_in_steps(cap, lines):
+    side = lax.axis_size("x")
+    copies = spread(cap, lax.all_gather(lines, "x"), side)
+    features = lax.all_to_all(copies, "y", split_axis=0, concat_axis=0, tiled=True)
+    return features.reshape(-1, *lines.shape)
+
+
+def gather_at_once(cap, lines):
+    copies = spread(cap, lines[None], lax.axis_size("y") * lax.axis_size("x"))
+    features = lax.all_to_all(copies, ("y", "x"), split_axis=0, concat_axis=0, tiled=True)
+    return features.reshape(-1, *lines.shape)
+
+
 def per_device(tokens, routes, gates, w_gate, w_up, w_down):
-    slots, side = lax.axis_size("z"), lax.axis_size("x")
-    shares = lax.axis_size("y") * side
+    slots = lax.axis_size("z")
+    shares = lax.axis_size("y") * lax.axis_size("x")
     count, top = routes.shape
     cap = min(count, 2 * count * top // slots)
     total = slots * cap * 3 // 2
     rows = slots * cap
-    plane = ("core", "y", "x")
-    along = range(side)
-    along_x = [[[c * shares + y * side + x for x in along] for y in along] for c in range(2)]
-    along_y = [[[c * shares + y * side + x for y in along] for x in along] for c in range(2)]
-    short = along_x[0] + along_y[1]
-    long = along_y[0] + along_x[1]
     outgoing, weights, own = call(
         functools.partial(dispatch_kernel, slots, cap),
         [(total, LANES), (6 * count, total), (3, *w_down.shape[1:])],
@@ -226,31 +237,37 @@
         hbm=(w_gate.swapaxes(1, 2), w_up.swapaxes(1, 2), w_down),
         scratch=[pltpu.SemaphoreType.DMA((3,))],
         limit=54,
-        keep=True,
+        keep=2,
     )
     other = lax.ppermute(own, "core", [(0, 1), (1, 0)])
-    incoming = exchange_z(outgoing, slots)
-    line = lax.all_gather(incoming, plane, axis_index_groups=short)
-    copies = call(
-        functools.partial(spread_kernel, cap), [(side, side, total, LANES)], line, limit=24
-    )
-    features = lax.all_to_all(
-        copies, plane, split_axis=0, concat_axis=0, axis_index_groups=long, tiled=True
-    )
-    partials = call(
-        ffn_kernel,
-        [(shares, total, LANES)],
-        features,
-        own,
-        other,
-        scratch=[pltpu.VMEM((rows, shares * SHARE), BF16)],
-        limit=32,
-        flops=2 * rows * shares * SHARE * 6 * SHARE,
-    )
-    landed = lax.all_to_all(partials, ("y", "x"), split_axis=0, concat_axis=0, tiled=True)
-    summed = call(functools.partial(sum_kernel, cap), [(total, LANES)], landed)
-    returned = exchange_z(summed, slots)
-    return call(combine_kernel, [(count, SHARE)], returned, weights)
+    outgoing, core = lax.optimization_barrier((outgoing, lax.axis_index("core")))
+    incoming, core = lax.optimization_barrier((exchange_z(outgoing, slots), core))
+    def finish(gather):
+        features = gather(cap, incoming)
+        partials = call(
+            ffn_kernel,
+            [(shares, total, LANES)],
+            features,
+            own,
+            hbm=(other,),
+            scratch=[
+                pltpu.VMEM((rows, shares * SHARE), BF16),
+                pltpu.VMEM(other.shape, BF16),
+                pltpu.SemaphoreType.DMA,
+            ],
+            limit=40,
+            flops=2 * rows * shares * SHARE * 6 * SHARE,
+        )
+        landed = lax.all_to_all(partials, ("y", "x"), split_axis=0, concat_axis=0, tiled=True)
+        summed = call(functools.partial(sum_kernel, cap), [(total, LANES)], landed)
+        returned = exchange_z(summed, slots)
+        return call(combine_kernel, [(count, SHARE)], returned, weights)
+
+    return lax.cond(
+        core == 0,
+        functools.partial(finish, gather_in_steps),
+        functools.partial(finish, gather_at_once),
+    )
 
 
 def split_mesh(mesh):

time: 171 us -> 175 us (1.023)
  Pallas kernels: 10.4 us -> 12.5 us
    all_to_all x2, blocking collectives: 51.1 us -> 44.8 us  [the longest x1 22.7 us: finish(): lax.all_to_all(partials, ('y', 'x'), split_axis=0, concat_axis=0, tiled=T...]
    all_to_all x2, blocking collectives: 92.7 us -> 97.8 us  [exchange_z(): lax.all_to_all(blocks, 'z', split_axis=0, concat_axis=0, tiled=True)]
    all_gather x1, blocking collectives: 12.9 us -> 15.4 us  [gather_in_steps(): copies = spread(cap, lax.all_gather(lines, 'x'), side)]
    pallas_call x5, Pallas kernels: 10.4 us -> 12.5 us  [call(): pl.pallas_call(kernel, out_shape=[(pltpu.VMEM if n == keep else jax.Shape...]
  transfers between devices with their start and end apart: 1 -> 1, of which waited for: 0 -> 0; matrix products, arithmetic and copies ran while one was open for 0% -> 0% of each run, Pallas kernels for 1% -> 0%
where the time goes in v4:
time: 175 us; the launch traced here: 173 us
  blocking collectives  158 us (90%)
  Pallas kernels  12.5 us (7%)
  starting transfers between devices  1.92 us (1%)
    all_to_all x2, blocking collectives, exchange_z(): lax.all_to_all(blocks, 'z', split_axis=0, concat_axis=0, tiled=True)  97.8 us
    all_to_all x1, blocking collectives, finish(): lax.all_to_all(partials, ('y', 'x'), split_axis=0, concat_axis=0, tiled=T...  22.7 us
    all_to_all x1, blocking collectives, gather_in_steps(): lax.all_to_all(copies, 'y', split_axis=0, concat_axis=0, tiled=True)  22.2 us
    all_gather x1, blocking collectives, gather_in_steps(): copies = spread(cap, lax.all_gather(lines, 'x'), side)  15.4 us
    pallas_call x5, Pallas kernels, call(): pl.pallas_call(kernel, out_shape=[(pltpu.VMEM if n == keep else jax.Shape...  12.5 us
  transfers between devices with their start and end apart: 1, of which 0 were waited for; matrix products, arithmetic and copies ran while one was open for 0% of the time, Pallas kernels for 0%

profile of v4, /device:TPU:6, one launch (start us, length us, event | category | flops | bytes accessed | tf_op | source)
XLA Modules:
  0.0 173.4 jit_solution(13968953678504088648)
XLA Ops:
  0.0 3.6 %shard_map.66 = (bf16[576,128]{1,0:T(8,128)(2,1)}, bf16[288,576]{1,0:T(8,128)(2,1)}, bf16[3,192,3072]{2,1,0:T(8,128)(2,1)S(1)}) custom-call(bf16[48,192]{1,0:T(8,128)(2,1)} %tokens_ref.1, s32[4,48]{1,0:T(4,128)} %bitcast.27, f32[4,48]{1,0:T(4,128)} %bitcast.28, bf16[1,192,3072]{2,1,0:T(8,128)(2,1)} %bitcast.24, bf16[1,192,3072]{2,1,0:T(8,128)(2,1)} %bitcast.25, ...), custom_call_target="tpu_custom_call" | custom-call | bytes 3558912 | tf_op jit(solution)/shard_map/pallas_call | solution.py:186
  3.6 1.9 %collective-permute-start = (bf16[3,192,3072]{2,1,0:T(8,128)(2,1)S(1)}, bf16[3,192,3072]{2,1,0:T(8,128)(2,1)}, u32[]{:S(2)}, u32[]{:S(2)}) collective-permute-start(bf16[3,192,3072]{2,1,0:T(8,128)(2,1)S(1)} %get-tuple-element.44), channel_id=1, source_target_pairs={{0,16},{16,0},{1,17},{17,1},{2,18},{18,2},{3,19},{19,3},{4,20},{20... | collective-permute-start | bytes 10616840 | tf_op jit(solution)/shard_map/ppermute | solution.py:242
  5.5 62.4 %all_to_all.35 = bf16[32,9,2,128]{3,2,1,0:T(2,128)(2,1)} all-to-all(bf16[32,9,2,128]{3,2,1,0:T(2,128)(2,1)} %bitcast.26), channel_id=1, replica_groups=mesh['z'=32,'core'=2,'y'=4,'x'=4] {'z'}, dimensions={0} | all-to-all | bytes 294912 | tf_op jit(solution)/shard_map/all_to_all | solution.py:203
  67.9 0.0 collective-permute-done
  67.9 104.8 %conditional.1 = (bf16[48,192]{1,0:T(8,128)(2,1)S(1)}) conditional(s32[]{:T(128)} %convert_element_type.3, (bf16[576,128]{1,0:T(8,128)(2,1)}, bf16[3,192,3072]{2,1,0:T(8,128)(2,1)S(1)}, bf16[3,192,3072]{2,1,0:T(8,128)(2,1)}, bf16[288,576]{1,0:T(8,128)(2,1)}) %tuple.20, (bf16[576,128]{1,0:T(8,128)(2,1)}, bf16[3,192,3072]{2,1,0:T(8,128)(2,1)S(1)}, ...), branch_computations={%region_0.0_spmd, %region_1.0_spmd} | conditional | flops 2717908992 | bytes 24662052 | solution.py:266
  67.9 15.4 %all-gather = bf16[2304,128]{1,0:T(8,128)(2,1)S(1)} all-gather(bf16[576,128]{1,0:T(8,128)(2,1)} %get-tuple-element.28), channel_id=2, replica_groups=mesh['z'=32,'core'=2,'y'=4,'x'=4] {'x'}, dimensions={0}, use_global_device_ids=true | all-gather | bytes 737280 | tf_op jit(solution)/shard_map/cond/branch_1_fun/all_gather | solution.py:213
  83.3 1.3 branch_1_fun.4
  84.6 22.2 %all_to_all.32 = bf16[4,4,576,128]{3,2,1,0:T(8,128)(2,1)S(1)} all-to-all(bf16[4,4,576,128]{3,2,1,0:T(8,128)(2,1)S(1)} %branch_1_fun.4), channel_id=1, replica_groups=mesh['z'=32,'core'=2,'y'=4,'x'=4] {'y'}, dimensions={0} | all-to-all | bytes 4718592 | tf_op jit(solution)/shard_map/cond/branch_1_fun/all_to_all | solution.py:214
  106.7 6.4 %branch_1_fun.5 = bf16[16,576,128]{2,1,0:T(8,128)(2,1)S(1)} custom-call(bf16[16,576,128]{2,1,0:T(8,128)(2,1)S(1)} %bitcast.15, bf16[3,192,3072]{2,1,0:T(8,128)(2,1)S(1)} %get-tuple-element.29.own_ref, bf16[3,192,3072]{2,1,0:T(8,128)(2,1)} %get-tuple-element.30.other_hbm), custom_call_target="tpu_custom_call" | custom-call | flops 2717908992 | bytes 9437184 | tf_op jit(solution)/shard_map/cond/branch_1_fun/pallas_call | solution.py:186
  113.1 22.7 %all_to_all.33.in_ref = bf16[16,576,128]{2,1,0:T(8,128)(2,1)S(1)} all-to-all(bf16[16,576,128]{2,1,0:T(8,128)(2,1)S(1)} %branch_1_fun.5), channel_id=1, replica_groups=mesh['z'=32,'core'=2,'y'=4,'x'=4] {'y','x'}, dimensions={0} | all-to-all | bytes 4718592 | tf_op jit(solution)/shard_map/cond/branch_1_fun/all_to_all | solution.py:261
  135.8 0.0 copy-start.1
  135.8 0.9 branch_1_fun.6
  136.7 35.4 %all_to_all.34 = bf16[32,9,2,128]{3,2,1,0:T(2,128)(2,1)S(1)} all-to-all(bf16[32,9,2,128]{3,2,1,0:T(2,128)(2,1)S(1)} %bitcast.18), channel_id=1, replica_groups=mesh['z'=32,'core'=2,'y'=4,'x'=4] {'z'}, dimensions={0} | all-to-all | bytes 294912 | tf_op jit(solution)/shard_map/cond/branch_1_fun/all_to_all | solution.py:203
  172.2 0.0 copy-done.1
  172.2 0.3 branch_1_fun.7
  172.7 0.0 copy-start.2
  172.8 0.6 copy-done.2
Async XLA Ops:
  3.6 64.3 %collective-permute-start = (bf16[3,192,3072]{2,1,0:T(8,128)(2,1)S(1)}, bf16[3,192,3072]{2,1,0:T(8,128)(2,1)}, u32[]{:S(2)}, u32[]{:S(2)}) collective-permute-start(bf16[3,192,3072]{2,1,0:T(8,128)(2,1)S(1)} %get-tuple-element.44), channel_id=1, source_target_pairs={{0,16},{16,0},{1,17},{17,1},{2,18},{18,2},{3,19},{19,3},{4,20},{20... | collective-permute-start | bytes 10616840 | tf_op jit(solution)/shard_map/ppermute | solution.py:242
  135.8 36.4 %copy-start.1 = (bf16[288,576]{1,0:T(8,128)(2,1)S(1)}, bf16[288,576]{1,0:T(8,128)(2,1)}, u32[]{:S(2)}) copy-start(bf16[288,576]{1,0:T(8,128)(2,1)} %get-tuple-element.31.weights_ref) | copy-start | bytes 995332 | tf_op jit(solution)/shard_map/cond
  172.7 0.6 copy-start.2

commit v5 on v3

--- a/solution.py
+++ b/solution.py
@@ -28,26 +28,51 @@
     return head, low, high
 
 
+def line_orders(total, cap):
+    half, group = cap // 2, total // 3
+    place, line_ids = iota((total, 1), 0), iota((total, total), 1)
+    kind, rest = place // group, place % group
+    source = rest // half * (3 * half) + rest % half + kind * half
+    block, line = place // (3 * half), place % (3 * half)
+    target = line // half * group + block * half + line % half
+    return [(index == line_ids).astype(F32).astype(BF16) for index in (source, target)]
+
+
 def dispatch_kernel(
     slots,
     cap,
-    tokens_ref,
-    routes_ref,
-    gates_ref,
+    tokens_hbm,
+    routes_hbm,
+    gates_hbm,
     w_gate_ref,
     w_up_ref,
     w_down_ref,
     out_ref,
     weights_ref,
     own_ref,
+    order_ref,
+    back_ref,
+    tokens_ref,
+    routes_ref,
+    gates_ref,
+    small_sems,
     sems,
 ):
+    small = [
+        pltpu.make_async_copy(source, target, small_sems.at[n])
+        for n, (source, target) in enumerate(
+            ((tokens_hbm, tokens_ref), (routes_hbm, routes_ref), (gates_hbm, gates_ref))
+        )
+    ]
     copies = [
         pltpu.make_async_copy(ref.at[0], own_ref.at[n], sems.at[n])
         for n, ref in enumerate((w_gate_ref, w_up_ref, w_down_ref))
     ]
-    for copy in copies:
+    for copy in small + copies:
         copy.start()
+    order_ref[...], back_ref[...] = line_orders(order_ref.shape[0], cap)
+    for copy in small:
+        copy.wait()
     odd = lax.rem(lax.axis_index("x"), 2) == 1
     count = tokens_ref.shape[0]
     top = routes_ref.shape[0]
@@ -100,22 +125,16 @@
         copy.wait()
 
 
-def spread_kernel(cap, in_ref, out_ref):
-    total = in_ref.shape[1]
-    half, group = cap // 2, total // 3
-    place = iota((total, 1), 0)
-    kind, rest = place // group, place % group
-    source = rest // half * (3 * half) + rest % half + kind * half
-    order = (source == iota((total, total), 1)).astype(F32).astype(BF16)
+def spread_kernel(in_ref, order_ref, out_ref):
     for share in range(in_ref.shape[0]):
-        lines = jnp.dot(order, in_ref[share], preferred_element_type=F32).astype(BF16)
+        lines = jnp.dot(order_ref[...], in_ref[share], preferred_element_type=F32).astype(BF16)
         for n in range(out_ref.shape[0]):
             out_ref[n, share] = lines
 
 
 def ffn_kernel(x_ref, own_ref, other_ref, out_ref, rows_ref):
     side = x_ref.shape[0]
-    first = lax.axis_index("core") == 0
+    first = lax.axis_index("core") == 1
 
     def block(n):
         y, x = n // side, n % side
@@ -158,17 +177,12 @@
         )
 
 
-def sum_kernel(cap, in_ref, out_ref):
-    total = in_ref.shape[1]
-    half, group = cap // 2, total // 3
+def sum_kernel(in_ref, order_ref, out_ref):
     acc = in_ref[0].astype(F32)
     for n in range(1, in_ref.shape[0]):
         acc = acc + in_ref[n].astype(F32)
-    place = iota((total, 1), 0)
-    block, line = place // (3 * half), place % (3 * half)
-    source = line // half * group + block * half + line % half
-    order = (source == iota((total, total), 1)).astype(F32).astype(BF16)
-    out_ref[...] = jnp.dot(order, acc.astype(BF16), preferred_element_type=F32).astype(BF16)
+    out = jnp.dot(order_ref[...], acc.astype(BF16), preferred_element_type=F32)
+    out_ref[...] = out.astype(BF16)
 
 
 def combine_kernel(in_ref, weights_ref, out_ref):
@@ -184,12 +198,15 @@
     out_ref[...] = out.astype(BF16)
 
 
-def call(kernel, shapes, *args, hbm=(), scratch=(), limit=16, flops=0, keep=False):
+def call(kernel, shapes, *args, hbm=(), scratch=(), limit=16, flops=0, keep=()):
     vmem = pl.BlockSpec(memory_space=pltpu.VMEM)
     size = sum(a.size * a.dtype.itemsize for a in (*args, *hbm))
     outs = pl.pallas_call(
         kernel,
-        out_shape=[(pltpu.VMEM if keep else jax.ShapeDtypeStruct)(shape, BF16) for shape in shapes],
+        out_shape=[
+            (pltpu.VMEM if n in keep else jax.ShapeDtypeStruct)(shape, BF16)
+            for n, shape in enumerate(shapes)
+        ],
         in_specs=[vmem] * len(args) + [pl.BlockSpec(memory_space=pltpu.HBM)] * len(hbm),
         out_specs=[vmem] * len(shapes),
         scratch_shapes=list(scratch),
@@ -215,25 +232,39 @@
     along = range(side)
     along_x = [[[c * shares + y * side + x for x in along] for y in along] for c in range(2)]
     along_y = [[[c * shares + y * side + x for y in along] for x in along] for c in range(2)]
-    short = along_x[0] + along_y[1]
-    long = along_y[0] + along_x[1]
-    outgoing, weights, own = call(
+    short = along_y[0] + along_x[1]
+    long = along_x[0] + along_y[1]
+    outgoing, weights, own, order, back = call(
         functools.partial(dispatch_kernel, slots, cap),
-        [(total, LANES), (6 * count, total), (3, *w_down.shape[1:])],
-        tokens,
-        routes.T,
-        gates.T,
-        hbm=(w_gate.swapaxes(1, 2), w_up.swapaxes(1, 2), w_down),
-        scratch=[pltpu.SemaphoreType.DMA((3,))],
+        [
+            (total, LANES),
+            (6 * count, total),
+            (3, *w_down.shape[1:]),
+            (total, total),
+            (total, total),
+        ],
+        hbm=(
+            tokens,
+            routes.T,
+            gates.T,
+            w_gate.swapaxes(1, 2),
+            w_up.swapaxes(1, 2),
+            w_down,
+        ),
+        scratch=[
+            pltpu.VMEM(tokens.shape, BF16),
+            pltpu.VMEM((top, count), jnp.int32),
+            pltpu.VMEM((top, count), F32),
+            pltpu.SemaphoreType.DMA((3,)),
+            pltpu.SemaphoreType.DMA((3,)),
+        ],
         limit=54,
-        keep=True,
+        keep=range(5),
     )
     other = lax.ppermute(own, "core", [(0, 1), (1, 0)])
     incoming = exchange_z(outgoing, slots)
     line = lax.all_gather(incoming, plane, axis_index_groups=short)
-    copies = call(
-        functools.partial(spread_kernel, cap), [(side, side, total, LANES)], line, limit=24
-    )
+    copies = call(spread_kernel, [(side, side, total, LANES)], line, order, limit=24)
     features = lax.all_to_all(
         copies, plane, split_axis=0, concat_axis=0, axis_index_groups=long, tiled=True
     )
@@ -248,7 +279,7 @@
         flops=2 * rows * shares * SHARE * 6 * SHARE,
     )
     landed = lax.all_to_all(partials, ("y", "x"), split_axis=0, concat_axis=0, tiled=True)
-    summed = call(functools.partial(sum_kernel, cap), [(total, LANES)], landed)
+    summed = call(sum_kernel, [(total, LANES)], landed, back)
     returned = exchange_z(summed, slots)
     return call(combine_kernel, [(count, SHARE)], returned, weights)
 

time: 171 us -> 170 us (level)
    all_to_all x1, blocking collectives: 22.2 us -> 20.4 us  [per_device(): lax.all_to_all(copies, plane, split_axis=0, concat_axis=0, axis_index_gro...]
where the time goes in v5:
time: 170 us; the launch traced here: 169 us
  blocking collectives  158 us (93%)
  Pallas kernels  9.38 us (6%)
  starting transfers between devices  1.92 us (1%)
    all_to_all x2, blocking collectives, exchange_z(): lax.all_to_all(blocks, 'z', split_axis=0, concat_axis=0, tiled=True)  93.8 us
    all_to_all x1, blocking collectives, per_device(): lax.all_to_all(partials, ('y', 'x'), split_axis=0, concat_axis=0, tiled=T...  29.9 us
    all_to_all x1, blocking collectives, per_device(): lax.all_to_all(copies, plane, split_axis=0, concat_axis=0, axis_index_gro...  20.4 us
    all_gather x1, blocking collectives, per_device(): line = lax.all_gather(incoming, plane, axis_index_groups=short)  13.4 us
    pallas_call x5, Pallas kernels, call(): pl.pallas_call(kernel, out_shape=[(pltpu.VMEM if n in keep else jax.Shape...  9.38 us
  transfers between devices with their start and end apart: 1, of which 0 were waited for; matrix products, arithmetic and copies ran while one was open for 0% of the time, Pallas kernels for 1%

profile of v5, /device:TPU:6, one launch (start us, length us, event | category | flops | bytes accessed | tf_op | source)
XLA Modules:
  0.0 168.9 jit_solution(9373035673817804382)
XLA Ops:
  0.0 2.5 %shard_map.64 = (bf16[576,128]{1,0:T(8,128)(2,1)S(1)}, bf16[288,576]{1,0:T(8,128)(2,1)S(1)}, bf16[3,192,3072]{2,1,0:T(8,128)(2,1)S(1)}, bf16[576,576]{1,0:T(8,128)(2,1)S(1)}, bf16[576,576]{1,0:T(8,128)(2,1)S(1)}) custom-call(bf16[48,192]{1,0:T(8,128)(2,1)} %tokens_hbm.1, s32[4,48]{1,0:T(4,128)} %bitcast.14, f32[4,48]{1,0:T(4,128)} %bitcast.15, ...), custom_call_target="tpu_custom_call" | custom-call | bytes 3558912 | tf_op jit(solution)/shard_map/pallas_call | solution.py:204
  2.5 1.9 %collective-permute-start = (bf16[3,192,3072]{2,1,0:T(8,128)(2,1)S(1)}, bf16[3,192,3072]{2,1,0:T(8,128)(2,1)S(1)}, u32[]{:S(2)}, u32[]{:S(2)}) collective-permute-start(bf16[3,192,3072]{2,1,0:T(8,128)(2,1)S(1)} %get-tuple-element.12.own_ref), channel_id=1, source_target_pairs={{0,16},{16,0},{1,17},{17,1},{2,18},{18,2},{3,19},{19,3},{4,20},{20... | collective-permute-start | bytes 10616840 | tf_op jit(solution)/shard_map/ppermute | solution.py:264
  4.4 62.1 %all_to_all.20 = bf16[32,9,2,128]{3,2,1,0:T(2,128)(2,1)S(1)} all-to-all(bf16[32,9,2,128]{3,2,1,0:T(2,128)(2,1)S(1)} %bitcast.10), channel_id=1, replica_groups=mesh['z'=32,'core'=2,'y'=4,'x'=4] {'z'}, dimensions={0} | all-to-all | bytes 294912 | tf_op jit(solution)/shard_map/all_to_all | solution.py:221
  66.4 13.4 %all_gather.3.in_ref = bf16[4,576,128]{2,1,0:T(8,128)(2,1)S(1)} all-gather(bf16[1,576,128]{2,1,0:T(8,128)(2,1)S(1)} %bitcast.13), channel_id=1, replica_groups={{0,4,8,12},{1,5,9,13},{2,6,10,14},{3,7,11,15},{16,17,18,19},{20,21,22,2..., dimensions={0}, use_global_device_ids=true | all-gather | bytes 737280 | tf_op jit(solution)/shard_map/all_gather | solution.py:266
  79.9 0.9 shard_map.65
  80.8 20.4 %all_to_all.21.x_ref = bf16[4,4,576,128]{3,2,1,0:T(8,128)(2,1)S(1)} all-to-all(bf16[4,4,576,128]{3,2,1,0:T(8,128)(2,1)S(1)} %shard_map.65), channel_id=1, replica_groups={{0,1,2,3},{4,5,6,7},{8,9,10,11},{12,13,14,15},{16,20,24,28},{17,21,25,2..., dimensions={0} | all-to-all | bytes 4718592 | tf_op jit(solution)/shard_map/all_to_all | solution.py:268
  101.2 0.0 collective-permute-done.other_ref
  101.2 4.5 %shard_map.66 = bf16[16,576,128]{2,1,0:T(8,128)(2,1)S(1)} custom-call(bf16[4,4,576,128]{3,2,1,0:T(8,128)(2,1)S(1)} %all_to_all.21.x_ref, bf16[3,192,3072]{2,1,0:T(8,128)(2,1)S(1)} %get-tuple-element.12.own_ref, bf16[3,192,3072]{2,1,0:T(8,128)(2,1)S(1)} %collective-permute-done.other_ref), custom_call_target="tpu_custom_call" | custom-call | flops 2717908992 | bytes 9437184 | tf_op jit(solution)/shard_map/pallas_call | solution.py:204
  105.7 29.9 %all_to_all.22.in_ref = bf16[16,576,128]{2,1,0:T(8,128)(2,1)S(1)} all-to-all(bf16[16,576,128]{2,1,0:T(8,128)(2,1)S(1)} %shard_map.66), channel_id=1, replica_groups=mesh['z'=32,'core'=2,'y'=4,'x'=4] {'y','x'}, dimensions={0} | all-to-all | bytes 4718592 | tf_op jit(solution)/shard_map/all_to_all | solution.py:281
  135.6 0.6 shard_map.67
  136.2 31.8 %all_to_all.23 = bf16[32,9,2,128]{3,2,1,0:T(2,128)(2,1)S(1)} all-to-all(bf16[32,9,2,128]{3,2,1,0:T(2,128)(2,1)S(1)} %bitcast.8), channel_id=1, replica_groups=mesh['z'=32,'core'=2,'y'=4,'x'=4] {'z'}, dimensions={0} | all-to-all | bytes 294912 | tf_op jit(solution)/shard_map/all_to_all | solution.py:221
  167.9 0.9 shard_map.68
Async XLA Ops:
  2.5 98.8 %collective-permute-start = (bf16[3,192,3072]{2,1,0:T(8,128)(2,1)S(1)}, bf16[3,192,3072]{2,1,0:T(8,128)(2,1)S(1)}, u32[]{:S(2)}, u32[]{:S(2)}) collective-permute-start(bf16[3,192,3072]{2,1,0:T(8,128)(2,1)S(1)} %get-tuple-element.12.own_ref), channel_id=1, source_target_pairs={{0,16},{16,0},{1,17},{17,1},{2,18},{18,2},{3,19},{19,3},{4,20},{20... | collective-permute-start | bytes 10616840 | tf_op jit(solution)/shard_map/ppermute | solution.py:264

commit v6 on v5

--- a/solution.py
+++ b/solution.py
@@ -134,7 +134,7 @@
 
 def ffn_kernel(x_ref, own_ref, other_ref, out_ref, rows_ref):
     side = x_ref.shape[0]
-    first = lax.axis_index("core") == 1
+    first = lax.axis_index("core") == 0
 
     def block(n):
         y, x = n // side, n % side
@@ -232,8 +232,8 @@
     along = range(side)
     along_x = [[[c * shares + y * side + x for x in along] for y in along] for c in range(2)]
     along_y = [[[c * shares + y * side + x for y in along] for x in along] for c in range(2)]
-    short = along_y[0] + along_x[1]
-    long = along_x[0] + along_y[1]
+    short = along_x[0] + along_y[1]
+    long = along_y[0] + along_x[1]
     outgoing, weights, own, order, back = call(
         functools.partial(dispatch_kernel, slots, cap),
         [

time: 170 us -> 170 us (level)
    all_to_all x1, blocking collectives: 20.4 us -> 22.2 us  [per_device(): lax.all_to_all(copies, plane, split_axis=0, concat_axis=0, axis_index_gro...]
where the time goes in v6:
time: 170 us; the launch traced here: 168 us
  blocking collectives  157 us (92%)
  Pallas kernels  9.38 us (6%)
  starting transfers between devices  1.92 us (1%)
    all_to_all x2, blocking collectives, exchange_z(): lax.all_to_all(blocks, 'z', split_axis=0, concat_axis=0, tiled=True)  92.7 us
    all_to_all x1, blocking collectives, per_device(): lax.all_to_all(partials, ('y', 'x'), split_axis=0, concat_axis=0, tiled=T...  28.9 us
    all_to_all x1, blocking collectives, per_device(): lax.all_to_all(copies, plane, split_axis=0, concat_axis=0, axis_index_gro...  22.2 us
    all_gather x1, blocking collectives, per_device(): line = lax.all_gather(incoming, plane, axis_index_groups=short)  12.9 us
    pallas_call x5, Pallas kernels, call(): pl.pallas_call(kernel, out_shape=[(pltpu.VMEM if n in keep else jax.Shape...  9.38 us
  transfers between devices with their start and end apart: 1, of which 0 were waited for; matrix products, arithmetic and copies ran while one was open for 0% of the time, Pallas kernels for 1%

profile of v6, /device:TPU:6, one launch (start us, length us, event | category | flops | bytes accessed | tf_op | source)
XLA Modules:
  0.0 168.1 jit_solution(15086134746047078243)
XLA Ops:
  0.0 2.5 %shard_map.64 = (bf16[576,128]{1,0:T(8,128)(2,1)S(1)}, bf16[288,576]{1,0:T(8,128)(2,1)S(1)}, bf16[3,192,3072]{2,1,0:T(8,128)(2,1)S(1)}, bf16[576,576]{1,0:T(8,128)(2,1)S(1)}, bf16[576,576]{1,0:T(8,128)(2,1)S(1)}) custom-call(bf16[48,192]{1,0:T(8,128)(2,1)} %tokens_hbm.1, s32[4,48]{1,0:T(4,128)} %bitcast.14, f32[4,48]{1,0:T(4,128)} %bitcast.15, ...), custom_call_target="tpu_custom_call" | custom-call | bytes 3558912 | tf_op jit(solution)/shard_map/pallas_call | solution.py:204
  2.5 1.9 %collective-permute-start = (bf16[3,192,3072]{2,1,0:T(8,128)(2,1)S(1)}, bf16[3,192,3072]{2,1,0:T(8,128)(2,1)S(1)}, u32[]{:S(2)}, u32[]{:S(2)}) collective-permute-start(bf16[3,192,3072]{2,1,0:T(8,128)(2,1)S(1)} %get-tuple-element.12.own_ref), channel_id=1, source_target_pairs={{0,16},{16,0},{1,17},{17,1},{2,18},{18,2},{3,19},{19,3},{4,20},{20... | collective-permute-start | bytes 10616840 | tf_op jit(solution)/shard_map/ppermute | solution.py:264
  4.4 62.1 %all_to_all.20 = bf16[32,9,2,128]{3,2,1,0:T(2,128)(2,1)S(1)} all-to-all(bf16[32,9,2,128]{3,2,1,0:T(2,128)(2,1)S(1)} %bitcast.10), channel_id=1, replica_groups=mesh['z'=32,'core'=2,'y'=4,'x'=4] {'z'}, dimensions={0} | all-to-all | bytes 294912 | tf_op jit(solution)/shard_map/all_to_all | solution.py:221
  66.4 12.9 %all_gather.3.in_ref = bf16[4,576,128]{2,1,0:T(8,128)(2,1)S(1)} all-gather(bf16[1,576,128]{2,1,0:T(8,128)(2,1)S(1)} %bitcast.13), channel_id=1, replica_groups={{0,1,2,3},{4,5,6,7},{8,9,10,11},{12,13,14,15},{16,20,24,28},{17,21,25,2..., dimensions={0}, use_global_device_ids=true | all-gather | bytes 737280 | tf_op jit(solution)/shard_map/all_gather | solution.py:266
  79.4 0.9 shard_map.65
  80.3 22.2 %all_to_all.21.x_ref = bf16[4,4,576,128]{3,2,1,0:T(8,128)(2,1)S(1)} all-to-all(bf16[4,4,576,128]{3,2,1,0:T(8,128)(2,1)S(1)} %shard_map.65), channel_id=1, replica_groups={{0,4,8,12},{1,5,9,13},{2,6,10,14},{3,7,11,15},{16,17,18,19},{20,21,22,2..., dimensions={0} | all-to-all | bytes 4718592 | tf_op jit(solution)/shard_map/all_to_all | solution.py:268
  102.5 0.0 collective-permute-done.other_ref
  102.5 4.5 %shard_map.66 = bf16[16,576,128]{2,1,0:T(8,128)(2,1)S(1)} custom-call(bf16[4,4,576,128]{3,2,1,0:T(8,128)(2,1)S(1)} %all_to_all.21.x_ref, bf16[3,192,3072]{2,1,0:T(8,128)(2,1)S(1)} %get-tuple-element.12.own_ref, bf16[3,192,3072]{2,1,0:T(8,128)(2,1)S(1)} %collective-permute-done.other_ref), custom_call_target="tpu_custom_call" | custom-call | flops 2717908992 | bytes 9437184 | tf_op jit(solution)/shard_map/pallas_call | solution.py:204
  106.9 28.9 %all_to_all.22.in_ref = bf16[16,576,128]{2,1,0:T(8,128)(2,1)S(1)} all-to-all(bf16[16,576,128]{2,1,0:T(8,128)(2,1)S(1)} %shard_map.66), channel_id=1, replica_groups=mesh['z'=32,'core'=2,'y'=4,'x'=4] {'y','x'}, dimensions={0} | all-to-all | bytes 4718592 | tf_op jit(solution)/shard_map/all_to_all | solution.py:281
  135.9 0.6 shard_map.67
  136.5 30.7 %all_to_all.23 = bf16[32,9,2,128]{3,2,1,0:T(2,128)(2,1)S(1)} all-to-all(bf16[32,9,2,128]{3,2,1,0:T(2,128)(2,1)S(1)} %bitcast.8), channel_id=1, replica_groups=mesh['z'=32,'core'=2,'y'=4,'x'=4] {'z'}, dimensions={0} | all-to-all | bytes 294912 | tf_op jit(solution)/shard_map/all_to_all | solution.py:221
  167.2 0.9 shard_map.68
Async XLA Ops:
  2.5 100.0 %collective-permute-start = (bf16[3,192,3072]{2,1,0:T(8,128)(2,1)S(1)}, bf16[3,192,3072]{2,1,0:T(8,128)(2,1)S(1)}, u32[]{:S(2)}, u32[]{:S(2)}) collective-permute-start(bf16[3,192,3072]{2,1,0:T(8,128)(2,1)S(1)} %get-tuple-element.12.own_ref), channel_id=1, source_target_pairs={{0,16},{16,0},{1,17},{17,1},{2,18},{18,2},{3,19},{19,3},{4,20},{20... | collective-permute-start | bytes 10616840 | tf_op jit(solution)/shard_map/ppermute | solution.py:264
